TPU v7x, 32 devices: a whole 2x2x4 slice. The times are simulated.
32 devices in a mesh: slab: 2 (over y), curve: 4 (over z), node: 2 (over x), sub: 2 (over core).
Axes of the slice: x: 2, y: 2, z: 4, core: 2. Of those that a mesh axis runs over, the one named last changes fastest.
Arguments:
- start_field: float32 [128, 16, 256], P(('slab', 'curve', 'sub')), parts along dimension 0, may hold values from -1 to 1
- neighbours: int32 [128, 6], P(('slab', 'curve', 'sub')), parts along dimension 0, may hold values from -1 to 63, as said below
Outputs:
- node_fields: float32 [2, 128, 16, 256], P('node', ('slab', 'curve', 'sub')), parts along dimension 1
- increments: float32 [4, 2], P('slab', 'node'), parts along dimension 0
There are 2 independent parts, one for each index of `slab`. A program takes and returns all parts, laid end to end along the dimension named above; each array names one. Nothing has to cross between parts.
Inputs may be any that keep to these rules, and one draw needn't show every extreme that they name: Leaf block c lies in layer c // 8 of the slab's first dimension; each layer holds 4 x 2 blocks visited in an order drawn per layer. The -x and +x neighbours lie in the adjacent layers, the others in the own layer. Where a block names b across a face, b names that block across the opposite face.
All inputs are finite; a program needn't handle non-finite values.
Results may differ from a plain program's by a relative error of at most 0.0001.
Values sent between devices are 32-bit elements; how exact they have to be, the bound alone decides.
No kernel may reach another device: no remote copies, remote signals or barrier semaphores. Data moves between devices by JAX's collectives and lax.ppermute only.
A program may use at most 64 MiB of HBM per device.

v0:
```python
import jax
import jax.numpy as jnp
import numpy as np
from jax import lax
from jax.sharding import PartitionSpec as P

SWEEPS = 2
JACOBI = 4


diffusion = 0.5
reaction = 1.0
opposite = (1, 0, 3, 2, 5, 4)


def padded_2(value, sides, width):
    for axis, dim in sides:
        peers, length = (lax.axis_size(axis), value.shape[dim])
        up = [(i, (i + 1) % peers) for i in range(peers - 1)]
        down = [(j, i) for i, j in up]
        last = lax.slice_in_dim(value, length - width, length, axis=dim)
        first = lax.slice_in_dim(value, 0, width, axis=dim)
        before = lax.ppermute(last, axis, up)
        after = lax.ppermute(first, axis, down)
        value = jnp.concatenate([before, value, after], axis=dim)
    return value


def legendre_value(order, place):
    before = 1.0
    current = place
    for degree in range(1, order):
        following = ((2 * degree + 1) * place * current - degree * before) / (degree + 1)
        before = current
        current = following
    return current


def radau_residue(node_count, moment):
    place = 2.0 * moment - 1.0
    return legendre_value(node_count, place) - legendre_value(node_count - 1, place)


def radau_tables(node_count):
    samples = 4000
    points = []
    for sample in range(samples - 1):
        left_end = sample / samples
        right_end = (sample + 1) / samples
        left_value = radau_residue(node_count, left_end)
        right_value = radau_residue(node_count, right_end)
        if left_value * right_value < 0.0:
            for halving in range(80):
                middle = 0.5 * (left_end + right_end)
                middle_value = radau_residue(node_count, middle)
                if left_value * middle_value <= 0.0:
                    right_end = middle
                else:
                    left_end = middle
                    left_value = middle_value
            points.append(0.5 * (left_end + right_end))
    points.append(1.0)
    table = []
    for row_node in range(node_count):
        table_row = []
        for col_node in range(node_count):
            factors = [1.0]
            for other_node in range(node_count):
                if other_node != col_node:
                    scale = 1.0 / (points[col_node] - points[other_node])
                    shifted = [0.0] + factors
                    product = [
                        shifted[place]
                        - points[other_node] * (factors[place] if place < len(factors) else 0.0)
                        for place in range(len(shifted))
                    ]
                    factors = [entry * scale for entry in product]
            integral = 0.0
            for power_index in range(len(factors)):
                integral = integral + factors[power_index] * points[row_node] ** (
                    power_index + 1
                ) / (power_index + 1)
            table_row.append(integral)
        table.append(table_row)
    return (np.array(table, dtype=np.float32), np.array(points, dtype=np.float32))


def face_stack(block_field):
    edge_cells = block_field.shape[1]
    block_count = block_field.shape[0]
    low_x = block_field[:, 0, :]
    high_x = block_field[:, -1, :]
    low_y = block_field[:, :, :edge_cells].reshape(block_count, -1)
    high_y = block_field[:, :, -edge_cells:].reshape(block_count, -1)
    low_z = block_field[:, :, 0::edge_cells].reshape(block_count, -1)
    high_z = block_field[:, :, edge_cells - 1 :: edge_cells].reshape(block_count, -1)
    return jnp.stack([low_x, high_x, low_y, high_y, low_z, high_z], axis=1)


def assemble(block_field, ghost_faces):
    edge_cells = block_field.shape[1]
    block_count = block_field.shape[0]
    plane_cells = block_field.shape[2]
    padded = jnp.concatenate(
        [ghost_faces[:, 0][:, None], block_field, ghost_faces[:, 1][:, None]], axis=1
    )
    totals = padded[:, :-2] + padded[:, 2:]
    below_y = jnp.concatenate(
        [
            ghost_faces[:, 2].reshape(block_count, edge_cells, edge_cells),
            block_field[:, :, :-edge_cells],
        ],
        axis=-1,
    )
    above_y = jnp.concatenate(
        [
            block_field[:, :, edge_cells:],
            ghost_faces[:, 3].reshape(block_count, edge_cells, edge_cells),
        ],
        axis=-1,
    )
    totals = totals + below_y + above_y
    within = jnp.arange(plane_cells, dtype=jnp.int32) % edge_cells
    lower_face = jnp.repeat(
        ghost_faces[:, 4].reshape(block_count, edge_cells, edge_cells), edge_cells, axis=-1
    )
    upper_face = jnp.repeat(
        ghost_faces[:, 5].reshape(block_count, edge_cells, edge_cells), edge_cells, axis=-1
    )
    totals = totals + jnp.where(within == 0, lower_face, jnp.roll(block_field, 1, axis=-1))
    totals = totals + jnp.where(
        within == edge_cells - 1, upper_face, jnp.roll(block_field, -1, axis=-1)
    )
    return totals


def shards(start_field, neighbours):
    node_count = lax.axis_size("node")
    node_index = lax.axis_index("node")
    weights, points = radau_tables(node_count)
    weight_table = jnp.asarray(weights)
    weight_row = weight_table[node_index]
    stiffness = jnp.float32(diffusion) * jnp.asarray(points)[node_index]
    block_count = start_field.shape[0]
    plane_cells = start_field.shape[2]
    total_cells = start_field.size * lax.axis_size(("curve", "sub"))
    local_rows = jnp.remainder(neighbours, block_count)
    sides = jnp.arange(6, dtype=jnp.int32)[None, :] + jnp.zeros((block_count, 1), jnp.int32)
    own_picks = jnp.arange(block_count, dtype=jnp.int32)[:, None] * 6 + sides
    remote_picks = 6 * block_count + sides * block_count + local_rows
    inside_picks = local_rows * 6 + jnp.asarray(opposite, dtype=jnp.int32)[None, :]
    chosen = jnp.where(sides < 2, remote_picks, inside_picks)
    face_picks = jnp.where(neighbours >= 0, chosen, own_picks)

    def neighbour_sum(block_field):
        own_faces = face_stack(block_field)
        outgoing = jnp.stack([own_faces[:, 0], own_faces[:, 1]], axis=0)
        received = padded_2(outgoing, ((("curve", "sub"), 0),), 1)
        face_table = jnp.concatenate(
            [own_faces.reshape(block_count * 6, plane_cells), received[0], received[3]], axis=0
        )
        ghost_faces = jnp.take(face_table, face_picks, axis=0)
        return assemble(block_field, ghost_faces)

    current = start_field
    norm_rows = []
    for sweep_index in range(SWEEPS):
        beside_all = neighbour_sum(current)
        laplace = beside_all - 6.0 * current
        forces = diffusion * laplace + reaction * current * (1.0 - current * current)
        shard_rows = lax.all_gather(forces[None], "node", axis=0, tiled=True)
        part_weights = lax.slice_in_dim(weight_row, 0, shard_rows.shape[0], axis=0)
        integral = jnp.zeros_like(forces) + jnp.sum(
            part_weights[:, None, None, None] * shard_rows, axis=0
        )
        right_side = start_field + integral - stiffness * laplace
        update = current
        neighbour_total = beside_all
        for jacobi_index in range(JACOBI):
            update = (right_side + stiffness * neighbour_total) / (1.0 + 6.0 * stiffness)
            if jacobi_index + 1 < JACOBI:
                neighbour_total = neighbour_sum(update)
        change = update - current
        local_square = jnp.sum(change * change)
        norm_rows.append(lax.psum(local_square, ("curve", "sub")))
        current = update
    totals = jnp.stack(norm_rows)
    increments = jnp.sqrt(totals / total_cells + 1e-06)
    return (current[None], increments[:, None])


def solution(mesh):
    placed = (P(("slab", "curve", "sub"), None, None), P(("slab", "curve", "sub"), None))
    return jax.shard_map(
        shards,
        mesh=mesh,
        in_specs=placed,
        out_specs=(P("node", ("slab", "curve", "sub"), None, None), P("slab", "node")),
        check_vma=False,
    )
```

profile of v0, /device:TPU:0, one launch (start us, length us, event | category | flops | bytes accessed | tf_op | source)
XLA Modules:
  0.0 129.2 jit_solution(8523332008971307980)
XLA Ops:
  0.6 1.0 copy.122
  1.7 2.4 %collective-permute-start = (f32[1,8,256]{2,1,0:T(8,128)S(1)}, f32[1,8,256]{2,1,0:T(8,128)S(1)}, u32[]{:S(2)}, u32[]{:S(2)}) collective-permute-start(f32[1,8,256]{2,1,0:T(8,128)S(1)} %get-tuple-element.108), channel_id=1, source_target_pairs={{0,1},{1,4},{4,5},{5,8},{8,9},{9,12},{12,13},{2,3},{3,6},{6,7},{7,... | collective-permute-start | bytes 24584 | tf_op jit(solution)/shard_map/ppermute | solution.py:23
  4.1 1.3 %collective-permute-start.1 = (f32[1,8,256]{2,1,0:T(8,128)S(1)}, f32[1,8,256]{2,1,0:T(8,128)S(1)}, u32[]{:S(2)}, u32[]{:S(2)}) collective-permute-start(f32[1,8,256]{2,1,0:T(8,128)S(1)} %get-tuple-element.109), channel_id=1, source_target_pairs={{1,0},{4,1},{5,4},{8,5},{9,8},{12,9},{13,12},{3,2},{6,3},{7,6},{10... | collective-permute-start | bytes 24584 | tf_op jit(solution)/shard_map/ppermute | solution.py:24
  7.7 0.7 copy-done.3
  11.0 0.6 gather_fusion
  13.9 5.9 %all-gather = f32[16,16,256]{2,0,1:T(8,128)S(1)} all-gather(f32[8,16,256]{2,0,1:T(8,128)S(1)} %get-tuple-element.18), channel_id=2, replica_groups=mesh['slab'=2,'curve'=4,'node'=2,'sub'=2] {'node'}, dimensions={0}, use_global_device_ids=true | all-gather | bytes 393216 | tf_op jit(solution)/shard_map/all_gather | solution.py:171
  21.6 1.3 %collective-permute-start.3 = (f32[1,8,256]{2,1,0:T(8,128)S(1)}, f32[1,8,256]{2,1,0:T(8,128)S(1)}, u32[]{:S(2)}, u32[]{:S(2)}) collective-permute-start(f32[1,8,256]{2,1,0:T(8,128)S(1)} %get-tuple-element.97), channel_id=1, source_target_pairs={{1,0},{4,1},{5,4},{8,5},{9,8},{12,9},{13,12},{3,2},{6,3},{7,6},{10... | collective-permute-start | bytes 24584 | tf_op jit(solution)/shard_map/ppermute | solution.py:24
  22.9 4.4 %collective-permute-start.2 = (f32[1,8,256]{2,1,0:T(8,128)S(1)}, f32[1,8,256]{2,1,0:T(8,128)S(1)}, u32[]{:S(2)}, u32[]{:S(2)}) collective-permute-start(f32[1,8,256]{2,1,0:T(8,128)S(1)} %get-tuple-element.98), channel_id=1, source_target_pairs={{0,1},{1,4},{4,5},{5,8},{8,9},{9,12},{12,13},{2,3},{3,6},{6,7},{7,... | collective-permute-start | bytes 24584 | tf_op jit(solution)/shard_map/ppermute | solution.py:23
  27.4 0.7 collective-permute-done.2
  32.6 5.1 %collective-permute-start.4 = (f32[1,8,256]{2,1,0:T(8,128)S(1)}, f32[1,8,256]{2,1,0:T(8,128)S(1)}, u32[]{:S(2)}, u32[]{:S(2)}) collective-permute-start(f32[1,8,256]{2,1,0:T(8,128)S(1)} %get-tuple-element.87), channel_id=1, source_target_pairs={{0,1},{1,4},{4,5},{5,8},{8,9},{9,12},{12,13},{2,3},{3,6},{6,7},{7,... | collective-permute-start | bytes 24584 | tf_op jit(solution)/shard_map/ppermute | solution.py:23
  37.7 1.3 %collective-permute-start.5 = (f32[1,8,256]{2,1,0:T(8,128)S(1)}, f32[1,8,256]{2,1,0:T(8,128)S(1)}, u32[]{:S(2)}, u32[]{:S(2)}) collective-permute-start(f32[1,8,256]{2,1,0:T(8,128)S(1)} %get-tuple-element.86), channel_id=1, source_target_pairs={{1,0},{4,1},{5,4},{8,5},{9,8},{12,9},{13,12},{3,2},{6,3},{7,6},{10... | collective-permute-start | bytes 24584 | tf_op jit(solution)/shard_map/ppermute | solution.py:24
  39.1 3.5 %collective-permute-done.5 = f32[1,8,256]{2,1,0:T(8,128)S(1)} collective-permute-done((f32[1,8,256]{2,1,0:T(8,128)S(1)}, f32[1,8,256]{2,1,0:T(8,128)S(1)}, u32[]{:S(2)}, u32[]{:S(2)}) %collective-permute-start.5) | collective-permute-done | bytes 8224 | tf_op jit(solution)/shard_map/ppermute | solution.py:24
  47.1 4.3 %collective-permute-start.6 = (f32[1,8,256]{2,1,0:T(8,128)S(1)}, f32[1,8,256]{2,1,0:T(8,128)S(1)}, u32[]{:S(2)}, u32[]{:S(2)}) collective-permute-start(f32[1,8,256]{2,1,0:T(8,128)S(1)} %get-tuple-element.76), channel_id=1, source_target_pairs={{0,1},{1,4},{4,5},{5,8},{8,9},{9,12},{12,13},{2,3},{3,6},{6,7},{7,... | collective-permute-start | bytes 24584 | tf_op jit(solution)/shard_map/ppermute | solution.py:23
  51.4 1.5 %collective-permute-start.7 = (f32[1,8,256]{2,1,0:T(8,128)S(1)}, f32[1,8,256]{2,1,0:T(8,128)S(1)}, u32[]{:S(2)}, u32[]{:S(2)}) collective-permute-start(f32[1,8,256]{2,1,0:T(8,128)S(1)} %get-tuple-element.75), channel_id=1, source_target_pairs={{1,0},{4,1},{5,4},{8,5},{9,8},{12,9},{13,12},{3,2},{6,3},{7,6},{10... | collective-permute-start | bytes 24584 | tf_op jit(solution)/shard_map/ppermute | solution.py:24
  52.9 1.5 %collective-permute-done.7 = f32[1,8,256]{2,1,0:T(8,128)S(1)} collective-permute-done((f32[1,8,256]{2,1,0:T(8,128)S(1)}, f32[1,8,256]{2,1,0:T(8,128)S(1)}, u32[]{:S(2)}, u32[]{:S(2)}) %collective-permute-start.7) | collective-permute-done | bytes 8224 | tf_op jit(solution)/shard_map/ppermute | solution.py:24
  58.9 3.8 %collective-permute-start.8 = (f32[1,8,256]{2,1,0:T(8,128)S(1)}, f32[1,8,256]{2,1,0:T(8,128)S(1)}, u32[]{:S(2)}, u32[]{:S(2)}) collective-permute-start(f32[1,8,256]{2,1,0:T(8,128)S(1)} %get-tuple-element.65), channel_id=1, source_target_pairs={{0,1},{1,4},{4,5},{5,8},{8,9},{9,12},{12,13},{2,3},{3,6},{6,7},{7,... | collective-permute-start | bytes 24584 | tf_op jit(solution)/shard_map/ppermute | solution.py:23
  62.8 1.3 %collective-permute-start.9 = (f32[1,8,256]{2,1,0:T(8,128)S(1)}, f32[1,8,256]{2,1,0:T(8,128)S(1)}, u32[]{:S(2)}, u32[]{:S(2)}) collective-permute-start(f32[1,8,256]{2,1,0:T(8,128)S(1)} %get-tuple-element.64), channel_id=1, source_target_pairs={{1,0},{4,1},{5,4},{8,5},{9,8},{12,9},{13,12},{3,2},{6,3},{7,6},{10... | collective-permute-start | bytes 24584 | tf_op jit(solution)/shard_map/ppermute | solution.py:24
  64.2 1.7 %collective-permute-done.9 = f32[1,8,256]{2,1,0:T(8,128)S(1)} collective-permute-done((f32[1,8,256]{2,1,0:T(8,128)S(1)}, f32[1,8,256]{2,1,0:T(8,128)S(1)}, u32[]{:S(2)}, u32[]{:S(2)}) %collective-permute-start.9) | collective-permute-done | bytes 8224 | tf_op jit(solution)/shard_map/ppermute | solution.py:24
  68.8 6.1 %all-gather.1 = f32[16,16,256]{2,0,1:T(8,128)S(1)} all-gather(f32[8,16,256]{2,0,1:T(8,128)S(1)} %get-tuple-element.14), channel_id=3, replica_groups=mesh['slab'=2,'curve'=4,'node'=2,'sub'=2] {'node'}, dimensions={0}, use_global_device_ids=true | all-gather | bytes 393216 | tf_op jit(solution)/shard_map/all_gather | solution.py:171
  76.6 2.7 %collective-permute-start.10 = (f32[1,8,256]{2,1,0:T(8,128)S(1)}, f32[1,8,256]{2,1,0:T(8,128)S(1)}, u32[]{:S(2)}, u32[]{:S(2)}) collective-permute-start(f32[1,8,256]{2,1,0:T(8,128)S(1)} %get-tuple-element.54), channel_id=1, source_target_pairs={{0,1},{1,4},{4,5},{5,8},{8,9},{9,12},{12,13},{2,3},{3,6},{6,7},{7,... | collective-permute-start | bytes 24584 | tf_op jit(solution)/shard_map/ppermute | solution.py:23
  79.3 1.3 %collective-permute-start.11 = (f32[1,8,256]{2,1,0:T(8,128)S(1)}, f32[1,8,256]{2,1,0:T(8,128)S(1)}, u32[]{:S(2)}, u32[]{:S(2)}) collective-permute-start(f32[1,8,256]{2,1,0:T(8,128)S(1)} %get-tuple-element.53), channel_id=1, source_target_pairs={{1,0},{4,1},{5,4},{8,5},{9,8},{12,9},{13,12},{3,2},{6,3},{7,6},{10... | collective-permute-start | bytes 24584 | tf_op jit(solution)/shard_map/ppermute | solution.py:24
  80.7 2.7 %collective-permute-done.11 = f32[1,8,256]{2,1,0:T(8,128)S(1)} collective-permute-done((f32[1,8,256]{2,1,0:T(8,128)S(1)}, f32[1,8,256]{2,1,0:T(8,128)S(1)}, u32[]{:S(2)}, u32[]{:S(2)}) %collective-permute-start.11) | collective-permute-done | bytes 8224 | tf_op jit(solution)/shard_map/ppermute | solution.py:24
  87.8 4.3 %collective-permute-start.12 = (f32[1,8,256]{2,1,0:T(8,128)S(1)}, f32[1,8,256]{2,1,0:T(8,128)S(1)}, u32[]{:S(2)}, u32[]{:S(2)}) collective-permute-start(f32[1,8,256]{2,1,0:T(8,128)S(1)} %get-tuple-element.43), channel_id=1, source_target_pairs={{0,1},{1,4},{4,5},{5,8},{8,9},{9,12},{12,13},{2,3},{3,6},{6,7},{7,... | collective-permute-start | bytes 24584 | tf_op jit(solution)/shard_map/ppermute | solution.py:23
  92.1 1.3 %collective-permute-start.13 = (f32[1,8,256]{2,1,0:T(8,128)S(1)}, f32[1,8,256]{2,1,0:T(8,128)S(1)}, u32[]{:S(2)}, u32[]{:S(2)}) collective-permute-start(f32[1,8,256]{2,1,0:T(8,128)S(1)} %get-tuple-element.42), channel_id=1, source_target_pairs={{1,0},{4,1},{5,4},{8,5},{9,8},{12,9},{13,12},{3,2},{6,3},{7,6},{10... | collective-permute-start | bytes 24584 | tf_op jit(solution)/shard_map/ppermute | solution.py:24
  93.5 1.7 %collective-permute-done.13 = f32[1,8,256]{2,1,0:T(8,128)S(1)} collective-permute-done((f32[1,8,256]{2,1,0:T(8,128)S(1)}, f32[1,8,256]{2,1,0:T(8,128)S(1)}, u32[]{:S(2)}, u32[]{:S(2)}) %collective-permute-start.13) | collective-permute-done | bytes 8224 | tf_op jit(solution)/shard_map/ppermute | solution.py:24
  99.7 4.1 %collective-permute-start.14 = (f32[1,8,256]{2,1,0:T(8,128)S(1)}, f32[1,8,256]{2,1,0:T(8,128)S(1)}, u32[]{:S(2)}, u32[]{:S(2)}) collective-permute-start(f32[1,8,256]{2,1,0:T(8,128)S(1)} %get-tuple-element.32), channel_id=1, source_target_pairs={{0,1},{1,4},{4,5},{5,8},{8,9},{9,12},{12,13},{2,3},{3,6},{6,7},{7,... | collective-permute-start | bytes 24584 | tf_op jit(solution)/shard_map/ppermute | solution.py:23
  103.8 1.3 %collective-permute-start.15 = (f32[1,8,256]{2,1,0:T(8,128)S(1)}, f32[1,8,256]{2,1,0:T(8,128)S(1)}, u32[]{:S(2)}, u32[]{:S(2)}) collective-permute-start(f32[1,8,256]{2,1,0:T(8,128)S(1)} %get-tuple-element.31), channel_id=1, source_target_pairs={{1,0},{4,1},{5,4},{8,5},{9,8},{12,9},{13,12},{3,2},{6,3},{7,6},{10... | collective-permute-start | bytes 24584 | tf_op jit(solution)/shard_map/ppermute | solution.py:24
  105.2 1.7 %collective-permute-done.15 = f32[1,8,256]{2,1,0:T(8,128)S(1)} collective-permute-done((f32[1,8,256]{2,1,0:T(8,128)S(1)}, f32[1,8,256]{2,1,0:T(8,128)S(1)}, u32[]{:S(2)}, u32[]{:S(2)}) %collective-permute-start.15) | collective-permute-done | bytes 8224 | tf_op jit(solution)/shard_map/ppermute | solution.py:24
  109.6 0.9 multiply_reduce_fusion.1
  110.5 0.7 copy.157
  111.2 16.2 %all-reduce = (f32[1,1]{0,1:T(1,128)}, f32[1,1]{0,1:T(1,128)}) all-reduce(f32[1,1]{0,1:T(1,128)} %bitcast.39, f32[1,1]{0,1:T(1,128)} %bitcast.38), channel_id=1, replica_groups=mesh['slab'=2,'curve'=4,'node'=2,'sub'=2] {'curve','sub'}, use_global_device_ids=true, to_apply=%region_5.7 | all-reduce | flops 2 | bytes 16 | tf_op jit(solution)/shard_map/psum | solution.py:185
  127.4 1.8 %fusion.62 = f32[2,1]{0,1:T(1,128)} fusion(f32[1,1]{0,1:T(1,128)} %get-tuple-element.9, f32[1,1]{0,1:T(1,128)} %get-tuple-element.10), kind=kLoop, calls=%fused_computation.208 | loop fusion | flops 6 | bytes 16 | tf_op jit(solution)/shard_map/sqrt | solution.py:188
  (346 shorter events, 36.3 us)
Async XLA Ops:
  0.6 4.8 %copy-start = (f32[8,16,256]{2,1,0:T(8,128)S(1)}, f32[8,16,256]{2,1,0:T(8,128)}, u32[]{:S(2)}) copy-start(f32[8,16,256]{2,1,0:T(8,128)} %param.7) | copy-start | bytes 393220
  1.7 9.2 %collective-permute-start = (f32[1,8,256]{2,1,0:T(8,128)S(1)}, f32[1,8,256]{2,1,0:T(8,128)S(1)}, u32[]{:S(2)}, u32[]{:S(2)}) collective-permute-start(f32[1,8,256]{2,1,0:T(8,128)S(1)} %get-tuple-element.108), channel_id=1, source_target_pairs={{0,1},{1,4},{4,5},{5,8},{8,9},{9,12},{12,13},{2,3},{3,6},{6,7},{7,... | collective-permute-start | bytes 24584 | tf_op jit(solution)/shard_map/ppermute | solution.py:23
  4.1 6.9 %collective-permute-start.1 = (f32[1,8,256]{2,1,0:T(8,128)S(1)}, f32[1,8,256]{2,1,0:T(8,128)S(1)}, u32[]{:S(2)}, u32[]{:S(2)}) collective-permute-start(f32[1,8,256]{2,1,0:T(8,128)S(1)} %get-tuple-element.109), channel_id=1, source_target_pairs={{1,0},{4,1},{5,4},{8,5},{9,8},{12,9},{13,12},{3,2},{6,3},{7,6},{10... | collective-permute-start | bytes 24584 | tf_op jit(solution)/shard_map/ppermute | solution.py:24
  6.8 0.7 copy-start.1
  6.8 0.7 copy-start.2
  7.7 0.7 copy-start.3
  8.4 0.7 copy-start.4
  21.6 5.8 %collective-permute-start.3 = (f32[1,8,256]{2,1,0:T(8,128)S(1)}, f32[1,8,256]{2,1,0:T(8,128)S(1)}, u32[]{:S(2)}, u32[]{:S(2)}) collective-permute-start(f32[1,8,256]{2,1,0:T(8,128)S(1)} %get-tuple-element.97), channel_id=1, source_target_pairs={{1,0},{4,1},{5,4},{8,5},{9,8},{12,9},{13,12},{3,2},{6,3},{7,6},{10... | collective-permute-start | bytes 24584 | tf_op jit(solution)/shard_map/ppermute | solution.py:24
  22.9 5.2 %collective-permute-start.2 = (f32[1,8,256]{2,1,0:T(8,128)S(1)}, f32[1,8,256]{2,1,0:T(8,128)S(1)}, u32[]{:S(2)}, u32[]{:S(2)}) collective-permute-start(f32[1,8,256]{2,1,0:T(8,128)S(1)} %get-tuple-element.98), channel_id=1, source_target_pairs={{0,1},{1,4},{4,5},{5,8},{8,9},{9,12},{12,13},{2,3},{3,6},{6,7},{7,... | collective-permute-start | bytes 24584 | tf_op jit(solution)/shard_map/ppermute | solution.py:23
  32.6 6.5 %collective-permute-start.4 = (f32[1,8,256]{2,1,0:T(8,128)S(1)}, f32[1,8,256]{2,1,0:T(8,128)S(1)}, u32[]{:S(2)}, u32[]{:S(2)}) collective-permute-start(f32[1,8,256]{2,1,0:T(8,128)S(1)} %get-tuple-element.87), channel_id=1, source_target_pairs={{0,1},{1,4},{4,5},{5,8},{8,9},{9,12},{12,13},{2,3},{3,6},{6,7},{7,... | collective-permute-start | bytes 24584 | tf_op jit(solution)/shard_map/ppermute | solution.py:23
  37.7 4.9 %collective-permute-start.5 = (f32[1,8,256]{2,1,0:T(8,128)S(1)}, f32[1,8,256]{2,1,0:T(8,128)S(1)}, u32[]{:S(2)}, u32[]{:S(2)}) collective-permute-start(f32[1,8,256]{2,1,0:T(8,128)S(1)} %get-tuple-element.86), channel_id=1, source_target_pairs={{1,0},{4,1},{5,4},{8,5},{9,8},{12,9},{13,12},{3,2},{6,3},{7,6},{10... | collective-permute-start | bytes 24584 | tf_op jit(solution)/shard_map/ppermute | solution.py:24
  47.1 5.9 %collective-permute-start.6 = (f32[1,8,256]{2,1,0:T(8,128)S(1)}, f32[1,8,256]{2,1,0:T(8,128)S(1)}, u32[]{:S(2)}, u32[]{:S(2)}) collective-permute-start(f32[1,8,256]{2,1,0:T(8,128)S(1)} %get-tuple-element.76), channel_id=1, source_target_pairs={{0,1},{1,4},{4,5},{5,8},{8,9},{9,12},{12,13},{2,3},{3,6},{6,7},{7,... | collective-permute-start | bytes 24584 | tf_op jit(solution)/shard_map/ppermute | solution.py:23
  51.4 3.1 %collective-permute-start.7 = (f32[1,8,256]{2,1,0:T(8,128)S(1)}, f32[1,8,256]{2,1,0:T(8,128)S(1)}, u32[]{:S(2)}, u32[]{:S(2)}) collective-permute-start(f32[1,8,256]{2,1,0:T(8,128)S(1)} %get-tuple-element.75), channel_id=1, source_target_pairs={{1,0},{4,1},{5,4},{8,5},{9,8},{12,9},{13,12},{3,2},{6,3},{7,6},{10... | collective-permute-start | bytes 24584 | tf_op jit(solution)/shard_map/ppermute | solution.py:24
  58.9 5.2 %collective-permute-start.8 = (f32[1,8,256]{2,1,0:T(8,128)S(1)}, f32[1,8,256]{2,1,0:T(8,128)S(1)}, u32[]{:S(2)}, u32[]{:S(2)}) collective-permute-start(f32[1,8,256]{2,1,0:T(8,128)S(1)} %get-tuple-element.65), channel_id=1, source_target_pairs={{0,1},{1,4},{4,5},{5,8},{8,9},{9,12},{12,13},{2,3},{3,6},{6,7},{7,... | collective-permute-start | bytes 24584 | tf_op jit(solution)/shard_map/ppermute | solution.py:23
  62.8 3.1 %collective-permute-start.9 = (f32[1,8,256]{2,1,0:T(8,128)S(1)}, f32[1,8,256]{2,1,0:T(8,128)S(1)}, u32[]{:S(2)}, u32[]{:S(2)}) collective-permute-start(f32[1,8,256]{2,1,0:T(8,128)S(1)} %get-tuple-element.64), channel_id=1, source_target_pairs={{1,0},{4,1},{5,4},{8,5},{9,8},{12,9},{13,12},{3,2},{6,3},{7,6},{10... | collective-permute-start | bytes 24584 | tf_op jit(solution)/shard_map/ppermute | solution.py:24
  76.6 4.1 %collective-permute-start.10 = (f32[1,8,256]{2,1,0:T(8,128)S(1)}, f32[1,8,256]{2,1,0:T(8,128)S(1)}, u32[]{:S(2)}, u32[]{:S(2)}) collective-permute-start(f32[1,8,256]{2,1,0:T(8,128)S(1)} %get-tuple-element.54), channel_id=1, source_target_pairs={{0,1},{1,4},{4,5},{5,8},{8,9},{9,12},{12,13},{2,3},{3,6},{6,7},{7,... | collective-permute-start | bytes 24584 | tf_op jit(solution)/shard_map/ppermute | solution.py:23
  79.3 4.1 %collective-permute-start.11 = (f32[1,8,256]{2,1,0:T(8,128)S(1)}, f32[1,8,256]{2,1,0:T(8,128)S(1)}, u32[]{:S(2)}, u32[]{:S(2)}) collective-permute-start(f32[1,8,256]{2,1,0:T(8,128)S(1)} %get-tuple-element.53), channel_id=1, source_target_pairs={{1,0},{4,1},{5,4},{8,5},{9,8},{12,9},{13,12},{3,2},{6,3},{7,6},{10... | collective-permute-start | bytes 24584 | tf_op jit(solution)/shard_map/ppermute | solution.py:24
  87.8 5.7 %collective-permute-start.12 = (f32[1,8,256]{2,1,0:T(8,128)S(1)}, f32[1,8,256]{2,1,0:T(8,128)S(1)}, u32[]{:S(2)}, u32[]{:S(2)}) collective-permute-start(f32[1,8,256]{2,1,0:T(8,128)S(1)} %get-tuple-element.43), channel_id=1, source_target_pairs={{0,1},{1,4},{4,5},{5,8},{8,9},{9,12},{12,13},{2,3},{3,6},{6,7},{7,... | collective-permute-start | bytes 24584 | tf_op jit(solution)/shard_map/ppermute | solution.py:23
  92.1 3.1 %collective-permute-start.13 = (f32[1,8,256]{2,1,0:T(8,128)S(1)}, f32[1,8,256]{2,1,0:T(8,128)S(1)}, u32[]{:S(2)}, u32[]{:S(2)}) collective-permute-start(f32[1,8,256]{2,1,0:T(8,128)S(1)} %get-tuple-element.42), channel_id=1, source_target_pairs={{1,0},{4,1},{5,4},{8,5},{9,8},{12,9},{13,12},{3,2},{6,3},{7,6},{10... | collective-permute-start | bytes 24584 | tf_op jit(solution)/shard_map/ppermute | solution.py:24
  99.7 5.5 %collective-permute-start.14 = (f32[1,8,256]{2,1,0:T(8,128)S(1)}, f32[1,8,256]{2,1,0:T(8,128)S(1)}, u32[]{:S(2)}, u32[]{:S(2)}) collective-permute-start(f32[1,8,256]{2,1,0:T(8,128)S(1)} %get-tuple-element.32), channel_id=1, source_target_pairs={{0,1},{1,4},{4,5},{5,8},{8,9},{9,12},{12,13},{2,3},{3,6},{6,7},{7,... | collective-permute-start | bytes 24584 | tf_op jit(solution)/shard_map/ppermute | solution.py:23
  103.8 3.1 %collective-permute-start.15 = (f32[1,8,256]{2,1,0:T(8,128)S(1)}, f32[1,8,256]{2,1,0:T(8,128)S(1)}, u32[]{:S(2)}, u32[]{:S(2)}) collective-permute-start(f32[1,8,256]{2,1,0:T(8,128)S(1)} %get-tuple-element.31), channel_id=1, source_target_pairs={{1,0},{4,1},{5,4},{8,5},{9,8},{12,9},{13,12},{3,2},{6,3},{7,6},{10... | collective-permute-start | bytes 24584 | tf_op jit(solution)/shard_map/ppermute | solution.py:24
where the time goes:
time: 130 us; the launch traced here: 129 us
  starting transfers between devices  41.7 us (32%)
  local copies, waits for them, and re-layouts  36.9 us (28%)
  blocking collectives  28.2 us (22%)
  waiting for transfers between devices  13.4 us (10%)
  other arithmetic  5.1 us (4%)
  between operations  3.89 us (3%)
    ppermute x8, starting transfers between devices, padded_2(): before = lax.ppermute(last, axis, up)  31.2 us
    psum x1, blocking collectives, shards(): norm_rows.append(lax.psum(local_square, ('curve', 'sub')))  16.2 us
    ppermute x8, waiting for transfers between devices, padded_2(): after = lax.ppermute(first, axis, down)  12.6 us
    all_gather x2, blocking collectives, shards(): shard_rows = lax.all_gather(forces[None], 'node', axis=0, tiled=True)  12 us
    ppermute x8, starting transfers between devices, padded_2(): after = lax.ppermute(first, axis, down)  10.5 us
    gather x16, local copies, waits for them, and re-layouts, neighbour_sum(): ghost_faces = jnp.take(face_table, face_picks, axis=0)  5.08 us
    unnamed x52, local copies, waits for them, and re-layouts  3.69 us
    reshape x8, local copies, waits for them, and re-layouts, assemble(): jnp.repeat(ghost_faces[:, 5].reshape(block_count, edge_cells, edge_cells)...  3.52 us
  transfers between devices with their start and end apart: 16, of which 7 were waited for; matrix products, arithmetic and copies ran while one was open for 2% of the time, Pallas kernels for 0%

commit v1 on v0

v1 whole, which is shorter than its diff:
```python
import functools

import jax
import jax.numpy as jnp
import numpy as np
from jax import lax
from jax.experimental import pallas as pl
from jax.experimental.pallas import tpu as pltpu
from jax.sharding import PartitionSpec as P

SWEEPS = 2
JACOBI = 4

diffusion = 0.5
reaction = 1.0
EDGE = 16
SPAN_Z = 2
LANES = 128
GROUP = SPAN_Z * EDGE
HALO = 8
PAD = 8
WIDTH = EDGE + 2 * HALO
ROWS = WIDTH + 2 * PAD
VMEM = pl.BlockSpec(memory_space=pltpu.VMEM)
SMEM = pl.BlockSpec(memory_space=pltpu.SMEM)


def legendre_value(order, place):
    before = 1.0
    current = place
    for degree in range(1, order):
        following = ((2 * degree + 1) * place * current - degree * before) / (degree + 1)
        before = current
        current = following
    return current


def radau_residue(node_count, moment):
    place = 2.0 * moment - 1.0
    return legendre_value(node_count, place) - legendre_value(node_count - 1, place)


def radau_tables(node_count):
    samples = 4000
    points = []
    for sample in range(samples - 1):
        left_end = sample / samples
        right_end = (sample + 1) / samples
        left_value = radau_residue(node_count, left_end)
        right_value = radau_residue(node_count, right_end)
        if left_value * right_value < 0.0:
            for halving in range(80):
                middle = 0.5 * (left_end + right_end)
                middle_value = radau_residue(node_count, middle)
                if left_value * middle_value <= 0.0:
                    right_end = middle
                else:
                    left_end = middle
                    left_value = middle_value
            points.append(0.5 * (left_end + right_end))
    points.append(1.0)
    table = []
    for row_node in range(node_count):
        table_row = []
        for col_node in range(node_count):
            factors = [1.0]
            for other_node in range(node_count):
                if other_node != col_node:
                    scale = 1.0 / (points[col_node] - points[other_node])
                    shifted = [0.0] + factors
                    product = [
                        shifted[place]
                        - points[other_node] * (factors[place] if place < len(factors) else 0.0)
                        for place in range(len(shifted))
                    ]
                    factors = [entry * scale for entry in product]
            integral = 0.0
            for power_index in range(len(factors)):
                integral = integral + factors[power_index] * points[row_node] ** (
                    power_index + 1
                ) / (power_index + 1)
            table_row.append(integral)
        table.append(table_row)
    return (np.array(table, dtype=np.float32), np.array(points, dtype=np.float32))


def slots_by_place(table):
    count = 8
    corner = jnp.int32(0)
    for slot in range(count):
        lowest = jnp.logical_and(table[slot, 2] < 0, table[slot, 4] < 0)
        corner = jnp.where(lowest, jnp.int32(slot), corner)
    slots = []
    for across_y in range(count // SPAN_Z):
        slots.append(corner)
        slots.append(table[corner, 5] & (count - 1))
        if across_y + 1 < count // SPAN_Z:
            corner = table[corner, 3] & (count - 1)
    return slots


def transpose_granules(values):
    lane = lax.broadcasted_iota(jnp.int32, (8, LANES), 1)
    for bit in (4, 2, 1):
        high = (lane // EDGE) & bit != 0
        out = list(values)
        for first in range(8):
            if first & bit == 0:
                low_value, high_value = values[first], values[first + bit]
                out[first] = jnp.where(high, pltpu.roll(high_value, EDGE * bit, 1), low_value)
                out[first + bit] = jnp.where(
                    high, high_value, pltpu.roll(low_value, LANES - EDGE * bit, 1)
                )
        values = out
    return values


def split_kernel(field, table, chip_half, far_half):
    sub = lax.axis_index("sub")
    slots = slots_by_place(table)
    for target, start in ((far_half, sub * 8), (chip_half, 8 - sub * 8)):
        rows = pl.ds(pl.multiple_of(start, 8), 8)
        for side in range(2):
            columns = slice(side * LANES, (side + 1) * LANES)
            values = transpose_granules([field[slot, rows, columns] for slot in slots])
            for row, value in enumerate(values):
                target[side * 8 + row] = value


def merge_kernel(planes, table, field):
    slots = slots_by_place(table)
    for half in range(2):
        rows = slice(half * 8, half * 8 + 8)
        for side in range(2):
            columns = slice(side * LANES, (side + 1) * LANES)
            values = transpose_granules([planes[side * 8 + row, rows] for row in range(8)])
            for slot, value in zip(slots, values):
                field[0, slot, rows, columns] = value


def chunks(level):
    count = -(-(WIDTH - 2 * level) // 8)
    first = (WIDTH - 8 * count) // 2
    return [PAD + first + 8 * piece for piece in range(count)]


def around(source, start, masks):
    at_low, at_high, first_group, last_group = masks
    rows = pl.ds(start, 8)
    below_rows = pl.ds(start - 1, 8)
    above_rows = pl.ds(start + 1, 8)
    first = source[0, rows]
    last = source[EDGE - 1, rows]
    before = jnp.where(first_group, first, pltpu.roll(last, GROUP, 1))
    beyond = jnp.where(last_group, last, pltpu.roll(first, LANES - GROUP, 1))
    current = first
    for j in range(EDGE):
        if j + 1 < EDGE:
            following = source[j + 1, rows]
        else:
            following = beyond
        total = (source[j, below_rows] + source[j, above_rows]) + (before + following)
        total = total + jnp.where(at_low, current, pltpu.roll(current, 1, 1))
        total = total + jnp.where(at_high, current, pltpu.roll(current, LANES - 1, 1))
        yield j, current, total
        before, current = current, following


def sweep_kernel(
    nodes, weights, points, chip_half, far_half, chip_got, far_got, planes, sums, base, state, right, after
):
    sub = lax.axis_index("sub")
    curve = lax.axis_index("curve")
    node = lax.axis_index("node")
    layer = curve * lax.axis_size("sub") + sub
    layers = lax.axis_size("curve") * lax.axis_size("sub")
    at_end = jnp.logical_or(layer == 0, layer == layers - 1)
    flip = sub == 1

    def place(source, normal, flipped):
        start = pl.multiple_of(PAD + jnp.where(flip, flipped, normal), 8)
        base[:, pl.ds(start, 8), :] = source[...]

    place(far_half, 8, 16)
    place(chip_half, 16, 8)
    place(chip_got, 24, 0)

    @pl.when(jnp.logical_not(at_end))
    def _():
        place(far_got, 0, 24)

    @pl.when(at_end)
    def _():
        start = PAD + jnp.where(flip, 24, 0)
        for row in range(8):
            base[:, pl.ds(start + 7 - row, 1), :] = far_half[:, row : row + 1, :]

    lane = lax.broadcasted_iota(jnp.int32, (8, LANES), 1)
    masks = (
        lane % GROUP == 0,
        lane % GROUP == GROUP - 1,
        lane < GROUP,
        lane >= LANES - GROUP,
    )
    stiffness = [np.float32(diffusion) * points[n] for n in range(nodes)]
    scales = [np.float32(1.0) / (np.float32(1.0) + np.float32(6.0) * a) for a in stiffness]
    whole = [np.float32(np.sum(weights[n].astype(np.float64))) for n in range(nodes)]

    for start in chunks(1):
        rows = pl.ds(start, 8)
        for j, value, total in around(base, start, masks):
            laplace = total - 6.0 * value
            force = diffusion * laplace + reaction * value * (1.0 - value * value)
            for n in range(nodes):
                right[n, j, rows] = (value + whole[n] * force - stiffness[n] * laplace) * scales[n]
                state[n, j, rows] = value + (whole[n] * scales[n]) * force
    for n in range(nodes):
        source, target = state.at[n], after.at[n]
        for level in range(2, JACOBI + 1):
            for start in chunks(level):
                rows = pl.ds(start, 8)
                for j, value, total in around(source, start, masks):
                    target[j, rows] = right[n, j, rows] + (stiffness[n] * scales[n]) * total
            source, target = target, source

    def own(values):
        chosen = jnp.float32(values[0])
        for n in range(1, nodes):
            chosen = jnp.where(node == n, jnp.float32(values[n]), chosen)
        return chosen

    own_stiffness = own(stiffness)
    own_scale = own(scales)
    own_weights = [own([weights[m, n] for m in range(nodes)]) for n in range(nodes)]
    fields = after if JACOBI % 2 == 0 else state
    spare = state if JACOBI % 2 == 0 else after
    for start in chunks(JACOBI + 1):
        rows = pl.ds(start, 8)
        for steps in zip(*[around(fields.at[n], start, masks) for n in range(nodes)]):
            j = steps[0][0]
            integral = base[j, rows]
            own_value = steps[0][1]
            own_laplace = None
            for n, (_, value, total) in enumerate(steps):
                laplace = total - 6.0 * value
                force = diffusion * laplace + reaction * value * (1.0 - value * value)
                integral = integral + own_weights[n] * force
                if n == 0:
                    own_laplace = laplace
                else:
                    own_value = jnp.where(node == n, value, own_value)
                    own_laplace = jnp.where(node == n, laplace, own_laplace)
            right[0, j, rows] = (integral - own_stiffness * own_laplace) * own_scale
            spare[0, j, rows] = (integral + (6.0 * own_stiffness) * own_value) * own_scale
    source, target = spare.at[0], spare.at[1]
    factor = own_stiffness * own_scale
    for level in range(JACOBI + 2, 2 * JACOBI):
        for start in chunks(level):
            rows = pl.ds(start, 8)
            for j, value, total in around(source, start, masks):
                target[j, rows] = right[0, j, rows] + factor * total
        source, target = target, source
    first_square = jnp.zeros((8, LANES), jnp.float32)
    second_square = jnp.zeros((8, LANES), jnp.float32)
    for start in chunks(2 * JACOBI):
        rows = pl.ds(start, 8)
        out_rows = pl.ds(start - PAD - HALO, 8)
        for j, value, total in around(source, start, masks):
            update = right[0, j, rows] + factor * total
            planes[j, out_rows] = update
            earlier = fields[node, j, rows]
            change = update - earlier
            second_square = second_square + change * change
            change = earlier - base[j, rows]
            first_square = first_square + change * change
    sums[0:1, :] = jnp.sum(first_square, axis=0, keepdims=True)
    sums[1:2, :] = jnp.sum(second_square, axis=0, keepdims=True)


def pairs_over(sizes, partner):
    pairs = []
    for index in np.ndindex(*sizes):
        other = partner(*[int(i) for i in index])
        if other is not None:
            pairs.append((int(np.ravel_multi_index(index, sizes)), int(np.ravel_multi_index(other, sizes))))
    return pairs


def shards(start_field, neighbours):
    nodes = lax.axis_size("node")
    axes = ("curve", "node", "sub")
    sizes = tuple(lax.axis_size(axis) for axis in axes)
    chips = sizes[0]
    weights, points = radau_tables(nodes)
    half = jax.ShapeDtypeStruct((EDGE, 8, LANES), jnp.float32)
    limit = pltpu.CompilerParams(vmem_limit_bytes=16 * 1024 * 1024)

    def across(curve, node, sub):
        if sub == 1 and curve + 1 < chips:
            return (curve + 1, node, 0)
        if sub == 0 and curve > 0:
            return (curve - 1, node, 1)
        return (curve, node ^ 1, sub) if node ^ 1 < nodes else None

    def beside(bit, swap):
        def partner(curve, node, sub):
            return (curve ^ bit, node, sub ^ swap)

        return partner

    def moved(value, partner):
        return lax.ppermute(value, axes, pairs_over(sizes, partner))

    chip_half, far_half = pl.pallas_call(
        split_kernel,
        out_shape=[half, half],
        in_specs=[VMEM, SMEM],
        out_specs=[VMEM, VMEM],
        compiler_params=limit,
    )(start_field, neighbours)
    far_got = moved(far_half, across)
    chip_got = moved(chip_half, beside(0, 1))
    planes, sums = pl.pallas_call(
        functools.partial(sweep_kernel, nodes, weights, points),
        out_shape=[
            jax.ShapeDtypeStruct((EDGE, EDGE, LANES), jnp.float32),
            jax.ShapeDtypeStruct((2, LANES), jnp.float32),
        ],
        in_specs=[VMEM] * 4,
        out_specs=[VMEM, VMEM],
        scratch_shapes=[
            pltpu.VMEM((EDGE, ROWS, LANES), jnp.float32),
            pltpu.VMEM((max(nodes, 2), EDGE, ROWS, LANES), jnp.float32),
            pltpu.VMEM((max(nodes, 2), EDGE, ROWS, LANES), jnp.float32),
            pltpu.VMEM((max(nodes, 2), EDGE, ROWS, LANES), jnp.float32),
        ],
        compiler_params=limit,
    )(chip_half, far_half, chip_got, far_got)
    field = pl.pallas_call(
        merge_kernel,
        out_shape=jax.ShapeDtypeStruct((1, 8, EDGE, EDGE * EDGE), jnp.float32),
        in_specs=[VMEM, SMEM],
        out_specs=VMEM,
        compiler_params=limit,
    )(planes, neighbours)
    sums = sums + moved(sums, beside(0, 1))
    bit = 1
    while bit < chips:
        sums = sums + moved(sums, beside(bit, 1))
        bit *= 2
    cells = start_field.size * chips * sizes[2]
    increments = jnp.sqrt(jnp.sum(sums, axis=1) / cells + 1e-06)
    return (field, increments[:, None])


def solution(mesh):
    placed = (P(("slab", "curve", "sub"), None, None), P(("slab", "curve", "sub"), None))
    return jax.shard_map(
        shards,
        mesh=mesh,
        in_specs=placed,
        out_specs=(P("node", ("slab", "curve", "sub"), None, None), P("slab", "node")),
        check_vma=False,
    )
```

time: 130 us -> 19.3 us (0.15)
  local copies, waits for them, and re-layouts: 36.9 us -> 1.58 us
  starting transfers between devices: 41.7 us -> 7.31 us
  blocking collectives: 28.2 us -> 0 us
  waiting for transfers between devices: 13.4 us -> 4.76 us
  other arithmetic: 5.1 us -> 0.65 us
  Pallas kernels: 0 us -> 4.13 us
  between operations: 3.89 us -> 0.65 us
    ppermute x16 -> x5, starting transfers between devices: 41.7 us -> 7.31 us  [moved(): return lax.ppermute(value, axes, pairs_over(sizes, partner))]
    psum x1 -> x0, blocking collectives: 16.2 us -> none  [shards(): norm_rows.append(lax.psum(local_square, ('curve', 'sub')))]
    all_gather x2 -> x0, blocking collectives: 12 us -> none  [shards(): shard_rows = lax.all_gather(forces[None], 'node', axis=0, tiled=True)]
    slice x84 -> x0, local copies, waits for them, and re-layouts: 8.68 us -> none  [the longest x15 2.85 us: face_stack(): block_field[:, :, edge_cells - 1::edge_cells].reshape(block_count, -1)]
    ppermute x16 -> x5, waiting for transfers between devices: 13.4 us -> 4.76 us  [moved(): return lax.ppermute(value, axes, pairs_over(sizes, partner))]
    reshape x24 -> x0, local copies, waits for them, and re-layouts: 7.1 us -> none  [the longest x8 3.52 us: assemble(): jnp.repeat(ghost_faces[:, 5].reshape(block_count, edge_cells, edge_cells)...]
    another operation x112 -> x0, local copies, waits for them, and re-layouts: 6.26 us -> none  [the longest x48 2.98 us: face_stack(): return jnp.stack([low_x, high_x, low_y, high_y, low_z, high_z], axis=1)]
    broadcast_in_dim x17 -> x0, local copies, waits for them, and re-layouts: 5.41 us -> none  [the longest x8 2.67 us: assemble(): jnp.repeat(ghost_faces[:, 4].reshape(block_count, edge_cells, edge_cells)...]
  transfers between devices with their start and end apart: 16 -> 5, of which waited for: 7 -> 3; matrix products, arithmetic and copies ran while one was open for 2% -> 0% of each run, Pallas kernels for 0% -> 8%
where the time goes in v1:
time: 19.3 us; the launch traced here: 19.1 us
  starting transfers between devices  7.31 us (38%)
  waiting for transfers between devices  4.76 us (25%)
  Pallas kernels  4.13 us (21%)
  local copies, waits for them, and re-layouts  1.58 us (8%)
  other arithmetic  0.65 us (3%)
  between operations  0.65 us (3%)
    ppermute x5, starting transfers between devices, moved(): return lax.ppermute(value, axes, pairs_over(sizes, partner))  7.31 us
    ppermute x5, waiting for transfers between devices, moved(): return lax.ppermute(value, axes, pairs_over(sizes, partner))  4.76 us
    pallas_call x1, Pallas kernels, shards(): pl.pallas_call(functools.partial(sweep_kernel, nodes, weights, points), o...  1.75 us
    unnamed x4, local copies, waits for them, and re-layouts  1.58 us
    pallas_call x1, Pallas kernels, shards(): pl.pallas_call(merge_kernel, out_shape=jax.ShapeDtypeStruct((1, 8, EDGE,...  1.49 us
    pallas_call x1, Pallas kernels, shards(): pl.pallas_call(split_kernel, out_shape=[half, half], in_specs=[VMEM, SMEM...  0.89 us
    sqrt x1, other arithmetic, shards(): increments = jnp.sqrt(jnp.sum(sums, axis=1) / cells + 1e-06)  0.53 us
  transfers between devices with their start and end apart: 5, of which 3 were waited for; matrix products, arithmetic and copies ran while one was open for 0% of the time, Pallas kernels for 8%

profile of v1, /device:TPU:0, one launch (start us, length us, event | category | flops | bytes accessed | tf_op | source)
XLA Modules:
  0.0 19.1 jit_solution(15558599536447063972)
XLA Ops:
  0.6 0.0 copy-start
  0.6 0.9 %copy-done = f32[8,16,256]{2,1,0:T(8,128)S(1)} copy-done((f32[8,16,256]{2,1,0:T(8,128)S(1)}, f32[8,16,256]{2,1,0:T(8,128)}, u32[]{:S(2)}) %copy-start) | copy-done | bytes 131096
  1.5 0.0 copy-start.1
  1.5 0.7 %copy-done.1 = s32[8,6]{1,0:T(8,128)S(1)} copy-done((s32[8,6]{1,0:T(8,128)S(1)}, s32[8,6]{1,0:T(8,128)}, u32[]{:S(2)}) %copy-start.1) | copy-done | bytes 216
  2.2 0.9 %shard_map.41 = (f32[16,8,128]{2,1,0:T(8,128)S(1)}, f32[16,8,128]{2,1,0:T(8,128)S(1)}) custom-call(f32[8,16,256]{2,1,0:T(8,128)S(1)} %copy-done, s32[8,6]{1,0:T(8,128)S(1)} %copy-done.1), custom_call_target="tpu_custom_call" | custom-call | tf_op jit(solution)/shard_map/pallas_call | solution.py:314
  3.1 0.5 %collective-permute-start = (f32[16,8,128]{2,1,0:T(8,128)S(1)}, f32[16,8,128]{2,1,0:T(8,128)S(1)}, u32[]{:S(2)}, u32[]{:S(2)}) collective-permute-start(f32[16,8,128]{2,1,0:T(8,128)S(1)} %get-tuple-element.6.chip_half), channel_id=1, source_target_pairs={{0,1},{1,0},{2,3},{3,2},{4,5},{5,4},{6,7},{7,6},{8,9},{9,8},{10,11... | collective-permute-start | bytes 196616 | tf_op jit(solution)/shard_map/ppermute | solution.py:312
  3.6 2.6 %collective-permute-start.1 = (f32[16,8,128]{2,1,0:T(8,128)S(1)}, f32[16,8,128]{2,1,0:T(8,128)S(1)}, u32[]{:S(2)}, u32[]{:S(2)}) collective-permute-start(f32[16,8,128]{2,1,0:T(8,128)S(1)} %get-tuple-element.7.far_half), channel_id=1, source_target_pairs={{0,2},{1,4},{2,0},{3,6},{4,1},{5,8},{6,3},{7,10},{8,5},{9,12},{10,... | collective-permute-start | bytes 196616 | tf_op jit(solution)/shard_map/ppermute | solution.py:312
  6.2 0.0 collective-permute-done.chip_got
  6.2 2.2 %collective-permute-done.1.far_got = f32[16,8,128]{2,1,0:T(8,128)S(1)} collective-permute-done((f32[16,8,128]{2,1,0:T(8,128)S(1)}, f32[16,8,128]{2,1,0:T(8,128)S(1)}, u32[]{:S(2)}, u32[]{:S(2)}) %collective-permute-start.1) | collective-permute-done | bytes 65568 | tf_op jit(solution)/shard_map/ppermute | solution.py:312
  8.4 1.7 %shard_map.42 = (f32[16,16,128]{2,1,0:T(8,128)S(1)}, f32[2,128]{1,0:T(2,128)S(1)}) custom-call(f32[16,8,128]{2,1,0:T(8,128)S(1)} %get-tuple-element.6.chip_half, f32[16,8,128]{2,1,0:T(8,128)S(1)} %get-tuple-element.7.far_half, f32[16,8,128]{2,1,0:T(8,128)S(1)} %collective-permute-done.chip_got, f32[16,8,128]{2,1,0:T(8,128)S(1)} %collective-permute-done.1.far_got), custom_call_target="tpu_custom_call" | custom-call | tf_op jit(solution)/shard_map/pallas_call | solution.py:323
  10.2 0.1 collective-permute-start.2
  10.3 1.1 %collective-permute-done.2 = f32[2,128]{1,0:T(2,128)S(1)} collective-permute-done((f32[2,128]{1,0:T(2,128)S(1)}, f32[2,128]{1,0:T(2,128)S(1)}, u32[]{:S(2)}, u32[]{:S(2)}) %collective-permute-start.2) | collective-permute-done | bytes 1056 | tf_op jit(solution)/shard_map/ppermute | solution.py:312
  11.4 1.5 %collective-permute-start.3 = (f32[2,128]{1,0:T(2,128)S(1)}, f32[2,128]{1,0:T(2,128)S(1)}, u32[]{:S(2)}, u32[]{:S(2)}) collective-permute-start(f32[2,128]{1,0:T(2,128)S(1)} %add.20), channel_id=1, source_target_pairs={{0,5},{1,4},{2,7},{3,6},{4,1},{5,0},{6,3},{7,2},{8,13},{9,12},{10,... | collective-permute-start | bytes 3080 | tf_op jit(solution)/shard_map/ppermute | solution.py:312
  12.9 1.5 %collective-permute-done.3 = f32[2,128]{1,0:T(2,128)S(1)} collective-permute-done((f32[2,128]{1,0:T(2,128)S(1)}, f32[2,128]{1,0:T(2,128)S(1)}, u32[]{:S(2)}, u32[]{:S(2)}) %collective-permute-start.3) | collective-permute-done | bytes 1056 | tf_op jit(solution)/shard_map/ppermute | solution.py:312
  14.4 2.5 %collective-permute-start.4 = (f32[2,128]{1,0:T(2,128)S(1)}, f32[2,128]{1,0:T(2,128)S(1)}, u32[]{:S(2)}, u32[]{:S(2)}) collective-permute-start(f32[2,128]{1,0:T(2,128)S(1)} %add.21), channel_id=1, source_target_pairs={{0,9},{1,8},{2,11},{3,10},{4,13},{5,12},{6,15},{7,14},{8,1},{9,0},... | collective-permute-start | bytes 3080 | tf_op jit(solution)/shard_map/ppermute | solution.py:312
  16.9 1.5 %shard_map.43 = f32[1,8,16,256]{3,2,1,0:T(8,128)} custom-call(f32[16,16,128]{2,1,0:T(8,128)S(1)} %get-tuple-element.8.planes, s32[8,6]{1,0:T(8,128)S(1)} %copy-done.1), custom_call_target="tpu_custom_call" | custom-call | tf_op jit(solution)/shard_map/pallas_call | solution.py:339
  18.4 0.0 collective-permute-done.4
  18.4 0.1 add_reduce_fusion
  18.6 0.5 %sqrt_bitcast_fusion = f32[2,1]{0,1:T(1,128)} fusion(f32[2]{0:T(128)S(1)} %add_reduce_fusion), kind=kLoop, calls=%fused_computation.1 | loop fusion | flops 4 | bytes 16 | tf_op jit(solution)/shard_map/sqrt | solution.py:352
  (2 shorter events, 0.0 us)
Async XLA Ops:
  0.6 0.9 %copy-start = (f32[8,16,256]{2,1,0:T(8,128)S(1)}, f32[8,16,256]{2,1,0:T(8,128)}, u32[]{:S(2)}) copy-start(f32[8,16,256]{2,1,0:T(8,128)} %field.1) | copy-start | bytes 393220
  1.5 0.7 %copy-start.1 = (s32[8,6]{1,0:T(8,128)S(1)}, s32[8,6]{1,0:T(8,128)}, u32[]{:S(2)}) copy-start(s32[8,6]{1,0:T(8,128)} %table.3) | copy-start | bytes 580
  3.1 3.1 %collective-permute-start = (f32[16,8,128]{2,1,0:T(8,128)S(1)}, f32[16,8,128]{2,1,0:T(8,128)S(1)}, u32[]{:S(2)}, u32[]{:S(2)}) collective-permute-start(f32[16,8,128]{2,1,0:T(8,128)S(1)} %get-tuple-element.6.chip_half), channel_id=1, source_target_pairs={{0,1},{1,0},{2,3},{3,2},{4,5},{5,4},{6,7},{7,6},{8,9},{9,8},{10,11... | collective-permute-start | bytes 196616 | tf_op jit(solution)/shard_map/ppermute | solution.py:312
  3.6 4.8 %collective-permute-start.1 = (f32[16,8,128]{2,1,0:T(8,128)S(1)}, f32[16,8,128]{2,1,0:T(8,128)S(1)}, u32[]{:S(2)}, u32[]{:S(2)}) collective-permute-start(f32[16,8,128]{2,1,0:T(8,128)S(1)} %get-tuple-element.7.far_half), channel_id=1, source_target_pairs={{0,2},{1,4},{2,0},{3,6},{4,1},{5,8},{6,3},{7,10},{8,5},{9,12},{10,... | collective-permute-start | bytes 196616 | tf_op jit(solution)/shard_map/ppermute | solution.py:312
  10.2 1.2 %collective-permute-start.2 = (f32[2,128]{1,0:T(2,128)S(1)}, f32[2,128]{1,0:T(2,128)S(1)}, u32[]{:S(2)}, u32[]{:S(2)}) collective-permute-start(f32[2,128]{1,0:T(2,128)S(1)} %get-tuple-element.9), channel_id=1, source_target_pairs={{0,1},{1,0},{2,3},{3,2},{4,5},{5,4},{6,7},{7,6},{8,9},{9,8},{10,11... | collective-permute-start | bytes 3080 | tf_op jit(solution)/shard_map/ppermute | solution.py:312
  11.4 3.0 %collective-permute-start.3 = (f32[2,128]{1,0:T(2,128)S(1)}, f32[2,128]{1,0:T(2,128)S(1)}, u32[]{:S(2)}, u32[]{:S(2)}) collective-permute-start(f32[2,128]{1,0:T(2,128)S(1)} %add.20), channel_id=1, source_target_pairs={{0,5},{1,4},{2,7},{3,6},{4,1},{5,0},{6,3},{7,2},{8,13},{9,12},{10,... | collective-permute-start | bytes 3080 | tf_op jit(solution)/shard_map/ppermute | solution.py:312
  14.4 4.0 %collective-permute-start.4 = (f32[2,128]{1,0:T(2,128)S(1)}, f32[2,128]{1,0:T(2,128)S(1)}, u32[]{:S(2)}, u32[]{:S(2)}) collective-permute-start(f32[2,128]{1,0:T(2,128)S(1)} %add.21), channel_id=1, source_target_pairs={{0,9},{1,8},{2,11},{3,10},{4,13},{5,12},{6,15},{7,14},{8,1},{9,0},... | collective-permute-start | bytes 3080 | tf_op jit(solution)/shard_map/ppermute | solution.py:312

commit v2 on v0

v2 whole, which is shorter than its diff:
```python
import functools

import jax
import jax.numpy as jnp
import numpy as np
from jax import lax
from jax.experimental import pallas as pl
from jax.experimental.pallas import tpu as pltpu
from jax.sharding import PartitionSpec as P

SWEEPS = 2
JACOBI = 4

diffusion = 0.5
reaction = 1.0
EDGE = 16
LANES = 128
CELLS = 16
SWAPS = ((4, 5), (2, 4), (1, 1), (8, 0))
VMEM = pl.BlockSpec(memory_space=pltpu.VMEM)


def legendre_value(order, place):
    before = 1.0
    current = place
    for degree in range(1, order):
        following = ((2 * degree + 1) * place * current - degree * before) / (degree + 1)
        before = current
        current = following
    return current


def radau_residue(node_count, moment):
    place = 2.0 * moment - 1.0
    return legendre_value(node_count, place) - legendre_value(node_count - 1, place)


def radau_tables(node_count):
    samples = 4000
    points = []
    for sample in range(samples - 1):
        left_end = sample / samples
        right_end = (sample + 1) / samples
        left_value = radau_residue(node_count, left_end)
        right_value = radau_residue(node_count, right_end)
        if left_value * right_value < 0.0:
            for halving in range(80):
                middle = 0.5 * (left_end + right_end)
                middle_value = radau_residue(node_count, middle)
                if left_value * middle_value <= 0.0:
                    right_end = middle
                else:
                    left_end = middle
                    left_value = middle_value
            points.append(0.5 * (left_end + right_end))
    points.append(1.0)
    table = []
    for row_node in range(node_count):
        table_row = []
        for col_node in range(node_count):
            factors = [1.0]
            for other_node in range(node_count):
                if other_node != col_node:
                    scale = 1.0 / (points[col_node] - points[other_node])
                    shifted = [0.0] + factors
                    product = [
                        shifted[place]
                        - points[other_node] * (factors[place] if place < len(factors) else 0.0)
                        for place in range(len(shifted))
                    ]
                    factors = [entry * scale for entry in product]
            integral = 0.0
            for power_index in range(len(factors)):
                integral = integral + factors[power_index] * points[row_node] ** (
                    power_index + 1
                ) / (power_index + 1)
            table_row.append(integral)
        table.append(table_row)
    return (np.array(table, dtype=np.float32), np.array(points, dtype=np.float32))


def swap_bits(values):
    lane = lax.broadcasted_iota(jnp.int32, (8, LANES), 1)
    for register_bit, lane_bit in SWAPS:
        shift = 1 << lane_bit
        high = (lane >> lane_bit) & 1 == 1
        out = list(values)
        for index in range(CELLS):
            if index & register_bit == 0:
                low_value, high_value = values[index], values[index | register_bit]
                out[index] = jnp.where(high, pltpu.roll(high_value, shift, 1), low_value)
                out[index | register_bit] = jnp.where(
                    high, high_value, pltpu.roll(low_value, LANES - shift, 1)
                )
        values = out
    return values


def cell_of(index):
    return ((index >> 1) & 3) * 4 + ((index & 1) << 1 | index >> 3)


def spread(source, store):
    values = [source[index & 7, :, (index >> 3) * LANES : (index >> 3) * LANES + LANES] for index in range(CELLS)]
    for index, value in enumerate(swap_bits(values)):
        store(cell_of(index), value)


def lane_of(slot, outer_j, outer_k):
    return (
        (outer_j & 1) << 6
        | (slot >> 2) << 5
        | ((slot >> 1) & 1) << 4
        | outer_k << 2
        | (slot & 1) << 1
        | outer_j >> 1
    )


def lane_routes(table, sub):
    lane = lax.broadcasted_iota(jnp.int32, (8, LANES), 1)
    row = lax.broadcasted_iota(jnp.int32, (8, LANES), 0)
    slot = ((lane >> 5) & 1) << 2 | ((lane >> 4) & 1) << 1 | (lane >> 1) & 1
    outer_j = (lane & 1) << 1 | lane >> 6
    outer_k = (lane >> 2) & 3
    named = []
    for face in range(6):
        column = jnp.broadcast_to(table[:, face : face + 1], (8, LANES))
        picked = jnp.sum(jnp.where(slot == row, column, 0), axis=0, keepdims=True)
        named.append(jnp.broadcast_to(picked, (8, LANES)))

    def inside(edge, face, within, wrapped):
        other = lane_of(named[face] & 7, *wrapped)
        other = jnp.where(named[face] < 0, LANES, other)
        return jnp.where(edge, other, lane_of(slot, *within))

    routes = [
        inside(outer_j == 0, 2, (outer_j - 1, outer_k), (3, outer_k)),
        inside(outer_j == 3, 3, (outer_j + 1, outer_k), (0, outer_k)),
        inside(outer_k == 0, 4, (outer_j, outer_k - 1), (outer_j, 3)),
        inside(outer_k == 3, 5, (outer_j, outer_k + 1), (outer_j, 0)),
    ]
    low = lane_of(named[0] & 7, outer_j, outer_k)
    high = lane_of(named[1] & 7, outer_j, outer_k)
    routes.append(jnp.where(sub == 0, high, low))
    routes.append(jnp.where(sub == 0, low, high))
    return routes


def picked(value, lanes):
    return jnp.take_along_axis(value, lanes, axis=1, mode="promise_in_bounds")


def halves_kernel(field, far_half, chip_half, far_done, chip_done):
    sub = lax.axis_index("sub")
    moves = []
    for target, start, done in (
        (far_half, sub * 8, far_done),
        (chip_half, 8 - sub * 8, chip_done),
    ):
        rows = pl.ds(pl.multiple_of(start, 8), 8)
        move = pltpu.make_async_copy(field.at[:, rows, :], target, done)
        move.start()
        moves.append(move)
    for move in moves:
        move.wait()


def merge_kernel(near, far, field):
    sub = lax.axis_index("sub")
    for planes, start in ((near, 8 - sub * 8), (far, sub * 8)):
        rows = pl.ds(pl.multiple_of(start, 8), 8)
        values = swap_bits([planes[cell_of(index)] for index in range(CELLS)])
        for index, value in enumerate(values):
            columns = slice((index >> 3) * LANES, (index >> 3) * LANES + LANES)
            field[0, index & 7, rows, columns] = value


def face_routes(routes):
    return [(route < LANES, route & (LANES - 1)) for route in routes[:4]]


def around(center, side_a, side_b, faces):
    def across(face, own, other):
        inner, lanes = faces[face]
        return jnp.where(inner, picked(other, lanes), own)

    cells = [center(cell) for cell in range(CELLS)]
    for cell in range(CELLS):
        value = cells[cell]
        inner_j, inner_k = cell // 4, cell % 4
        total = side_a(cell) + side_b(cell)
        below = cells[cell - 4] if inner_j > 0 else across(0, value, cells[cell + 12])
        above = cells[cell + 4] if inner_j < 3 else across(1, value, cells[cell - 12])
        before = cells[cell - 1] if inner_k > 0 else across(2, value, cells[cell + 3])
        behind = cells[cell + 1] if inner_k < 3 else across(3, value, cells[cell - 3])
        yield cell, value, (total + (below + above)) + (before + behind)


def around_at(source, start, step, faces):
    return around(
        lambda cell: source[cell, pl.ds(start, 8)],
        lambda cell: source[cell, pl.ds(start - step, 8)],
        lambda cell: source[cell, pl.ds(start + step, 8)],
        faces,
    )


class Scheme:
    def __init__(self, nodes, weights, points):
        one, six = np.float32(1.0), np.float32(6.0)
        self.nodes = nodes
        self.weights = weights
        self.stiffness = [np.float32(diffusion) * points[n] for n in range(nodes)]
        self.scales = [one / (one + six * a) for a in self.stiffness]
        self.whole = [np.float32(np.sum(weights[n].astype(np.float64))) for n in range(nodes)]
        self.count = 5 * nodes + 5

    def field(self, level, node=0):
        if level == 0:
            return 0
        if level <= JACOBI:
            return 1 + (level - 1) * self.nodes + node
        return JACOBI * self.nodes + level - JACOBI

    def right(self, sweep, node=0):
        return JACOBI * self.nodes + JACOBI + (node if sweep == 0 else self.nodes)

    def own(self, node, values):
        chosen = jnp.float32(values[0])
        for n in range(1, self.nodes):
            chosen = jnp.where(node == n, jnp.float32(values[n]), chosen)
        return chosen

    def first_step(self, value, total):
        laplace = total - 6.0 * value
        force = diffusion * laplace + reaction * value * (1.0 - value * value)
        for n in range(self.nodes):
            right = (value + self.whole[n] * force - self.stiffness[n] * laplace) * self.scales[n]
            yield n, right, value + (self.whole[n] * self.scales[n]) * force

    def second_step(self, node, start, steps):
        stiffness = self.own(node, self.stiffness)
        scale = self.own(node, self.scales)
        integral = start
        own_value, own_laplace = None, None
        for n, (_, value, total) in enumerate(steps):
            laplace = total - 6.0 * value
            force = diffusion * laplace + reaction * value * (1.0 - value * value)
            weight = self.own(node, [self.weights[m, n] for m in range(self.nodes)])
            integral = integral + weight * force
            own_value = value if n == 0 else jnp.where(node == n, value, own_value)
            own_laplace = laplace if n == 0 else jnp.where(node == n, laplace, own_laplace)
        right = (integral - stiffness * own_laplace) * scale
        return right, (integral + (6.0 * stiffness) * own_value) * scale

    def factor(self, node, sweep, n):
        if sweep == 0:
            return self.stiffness[n] * self.scales[n]
        return self.own(node, self.stiffness) * self.own(node, self.scales)


def near_kernel(scheme, chip_half, far_half, chip_got, table, edges, planes, sums, lanes, state):
    sub = lax.axis_index("sub")
    node = lax.axis_index("node")
    nodes = scheme.nodes
    routes = lane_routes(table, sub)
    for index, route in enumerate(routes):
        lanes[index] = route
    faces = face_routes(routes)
    low_half = pl.ds(pl.multiple_of(sub * 16, 8), 8)
    chip_half_rows = pl.ds(8, 8)
    high_half = pl.ds(pl.multiple_of(16 - sub * 16, 8), 8)

    def store_far(cell, value):
        state[0, cell, low_half] = value
        edges[0, 0, cell] = value
        edges[1, 0, cell] = value

    def store_chip(cell, value):
        state[0, cell, chip_half_rows] = value

    def store_got(cell, value):
        state[0, cell, high_half] = picked(value, routes[4])

    spread(far_half, store_far)
    spread(chip_half, store_chip)
    spread(chip_got, store_got)

    span = EDGE + 8

    def starts(level):
        count = -(-(span - 2 * level) // 8)
        if count == 1:
            return [level]
        return [level + round(piece * (span - 2 * level - 8) / (count - 1)) for piece in range(count)]

    def keep(index, level, start, cell, value):
        state[index, cell, pl.ds(start, 8)] = value
        if start == level:
            edges[0, index, cell] = value
        if start == span - 8 - level:
            edges[1, index, cell] = value

    for start in starts(1):
        for cell, value, total in around_at(state.at[0], start, 1, faces):
            for n, right, update in scheme.first_step(value, total):
                keep(scheme.right(0, n), 1, start, cell, right)
                keep(scheme.field(1, n), 1, start, cell, update)
    for level in range(2, JACOBI + 1):
        for start in starts(level):
            for n in range(nodes):
                factor = scheme.factor(node, 0, n)
                for cell, value, total in around_at(state.at[scheme.field(level - 1, n)], start, 1, faces):
                    right = state[scheme.right(0, n), cell, pl.ds(start, 8)]
                    keep(scheme.field(level, n), level, start, cell, right + factor * total)
    level = JACOBI + 1
    for start in starts(level):
        sources = [state.at[scheme.field(JACOBI, n)] for n in range(nodes)]
        for steps in zip(*[around_at(source, start, 1, faces) for source in sources]):
            cell = steps[0][0]
            right, update = scheme.second_step(node, state[0, cell, pl.ds(start, 8)], steps)
            keep(scheme.right(1), level, start, cell, right)
            keep(scheme.field(level), level, start, cell, update)
    factor = scheme.factor(node, 1, 0)
    for level in range(JACOBI + 2, 2 * JACOBI):
        for start in starts(level):
            for cell, value, total in around_at(state.at[scheme.field(level - 1)], start, 1, faces):
                right = state[scheme.right(1), cell, pl.ds(start, 8)]
                keep(scheme.field(level), level, start, cell, right + factor * total)
    first_square = jnp.zeros((8, LANES), jnp.float32)
    second_square = jnp.zeros((8, LANES), jnp.float32)
    start = 2 * JACOBI
    rows = pl.ds(start, 8)
    earlier_place = scheme.field(JACOBI) + node
    for cell, value, total in around_at(state.at[scheme.field(start - 1)], start, 1, faces):
        update = state[scheme.right(1), cell, rows] + factor * total
        planes[cell] = update
        earlier = state[earlier_place, cell, rows]
        change = update - earlier
        second_square = second_square + change * change
        change = earlier - state[0, cell, rows]
        first_square = first_square + change * change
    sums[0] = first_square
    sums[1] = second_square


def far_kernel(scheme, far_got, edges, near_sums, lanes, planes, sums, state):
    sub = lax.axis_index("sub")
    curve = lax.axis_index("curve")
    node = lax.axis_index("node")
    nodes = scheme.nodes
    faces = face_routes([lanes[index] for index in range(4)])
    toward = 1 - 2 * sub
    at_end = jnp.where(sub == 0, curve == 0, curve == lax.axis_size("curve") - 1)
    beside = pl.ds(pl.multiple_of(8 + 8 * toward, 8), 8)
    new = pl.ds(8, 8)
    for index in range(scheme.count):
        for cell in range(CELLS):
            state[index, cell, beside] = edges[sub, index, cell]

    def store_far(cell, value):
        state[0, cell, new] = picked(value, lanes[5])

    spread(far_got, store_far)

    @pl.when(at_end)
    def _():
        for row in range(8):
            state[0, :, 15 - row : 16 - row, :] = edges[sub, 0, :, row : row + 1, :]

    def shifted(levels):
        return pl.ds(8 + toward * levels, 8)

    def ring(index):
        source = state.at[index]
        return around(
            lambda cell: source[cell, shifted(1)],
            lambda cell: source[cell, new],
            lambda cell: source[cell, shifted(2)],
            faces,
        )

    def write(pending):
        for index, cell, value in pending:
            state[index, cell, new] = value

    pending = []
    for cell, value, total in ring(0):
        for n, right, update in scheme.first_step(value, total):
            pending.append((scheme.right(0, n), cell, right))
            pending.append((scheme.field(1, n), cell, update))
    write(pending)
    for level in range(2, JACOBI + 1):
        pending = []
        for n in range(nodes):
            factor = scheme.factor(node, 0, n)
            for cell, value, total in ring(scheme.field(level - 1, n)):
                right = state[scheme.right(0, n), cell, shifted(level - 1)]
                pending.append((scheme.field(level, n), cell, right + factor * total))
        write(pending)
    level = JACOBI + 1
    pending = []
    for steps in zip(*[ring(scheme.field(JACOBI, n)) for n in range(nodes)]):
        cell = steps[0][0]
        right, update = scheme.second_step(node, state[0, cell, shifted(level)], steps)
        pending.append((scheme.right(1), cell, right))
        pending.append((scheme.field(level), cell, update))
    write(pending)
    factor = scheme.factor(node, 1, 0)
    for level in range(JACOBI + 2, 2 * JACOBI):
        pending = []
        for cell, value, total in ring(scheme.field(level - 1)):
            right = state[scheme.right(1), cell, shifted(level - JACOBI - 1)]
            pending.append((scheme.field(level), cell, right + factor * total))
        write(pending)
    first_square = near_sums[0]
    second_square = near_sums[1]
    level = 2 * JACOBI
    for cell, value, total in ring(scheme.field(level - 1)):
        update = state[scheme.right(1), cell, shifted(JACOBI - 1)] + factor * total
        planes[cell] = update
        earlier = state[scheme.field(JACOBI) + node, cell, shifted(JACOBI)]
        change = update - earlier
        second_square = second_square + change * change
        change = earlier - state[0, cell, shifted(level)]
        first_square = first_square + change * change
    sums[0:1, :] = jnp.sum(first_square, axis=0, keepdims=True)
    sums[1:2, :] = jnp.sum(second_square, axis=0, keepdims=True)


def pairs_over(sizes, partner):
    pairs = []
    for index in np.ndindex(*sizes):
        other = partner(*[int(i) for i in index])
        if other is not None:
            pairs.append((int(np.ravel_multi_index(index, sizes)), int(np.ravel_multi_index(other, sizes))))
    return pairs


def shards(start_field, neighbours):
    nodes = lax.axis_size("node")
    axes = ("curve", "node", "sub")
    sizes = tuple(lax.axis_size(axis) for axis in axes)
    chips = sizes[0]
    scheme = Scheme(nodes, *radau_tables(nodes))
    half = jax.ShapeDtypeStruct((8, 8, EDGE * EDGE), jnp.float32)
    planes = jax.ShapeDtypeStruct((CELLS, 8, LANES), jnp.float32)
    limit = pltpu.CompilerParams(vmem_limit_bytes=24 * 1024 * 1024)

    def across(curve, node, sub):
        if sub == 1 and curve + 1 < chips:
            return (curve + 1, node, 0)
        if sub == 0 and curve > 0:
            return (curve - 1, node, 1)
        return (curve, node ^ 1, sub) if node ^ 1 < nodes else None

    def beside(bit, swap):
        def partner(curve, node, sub):
            return (curve ^ bit, node, sub ^ swap)

        return partner

    def moved(value, partner):
        return lax.ppermute(value, axes, pairs_over(sizes, partner))

    far_half, chip_half = pl.pallas_call(
        halves_kernel,
        out_shape=[half, half],
        in_specs=[pl.BlockSpec(memory_space=pltpu.HBM)],
        out_specs=[VMEM, VMEM],
        scratch_shapes=[pltpu.SemaphoreType.DMA, pltpu.SemaphoreType.DMA],
        compiler_params=limit,
    )(start_field)
    far_got = moved(far_half, across)
    chip_got = moved(chip_half, beside(0, 1))
    edges, near_planes, near_sums, lanes = pl.pallas_call(
        functools.partial(near_kernel, scheme),
        out_shape=[
            jax.ShapeDtypeStruct((2, scheme.count, CELLS, 8, LANES), jnp.float32),
            planes,
            jax.ShapeDtypeStruct((2, 8, LANES), jnp.float32),
            jax.ShapeDtypeStruct((6, 8, LANES), jnp.int32),
        ],
        in_specs=[VMEM] * 4,
        out_specs=[VMEM] * 4,
        scratch_shapes=[pltpu.VMEM((scheme.count, CELLS, EDGE + 8, LANES), jnp.float32)],
        compiler_params=limit,
        cost_estimate=pl.CostEstimate(flops=8_000_000, bytes_accessed=2_000_000, transcendentals=0),
    )(chip_half, far_half, chip_got, neighbours)
    far_planes, sums = pl.pallas_call(
        functools.partial(far_kernel, scheme),
        out_shape=[planes, jax.ShapeDtypeStruct((2, LANES), jnp.float32)],
        in_specs=[VMEM] * 4,
        out_specs=[VMEM, VMEM],
        scratch_shapes=[pltpu.VMEM((scheme.count, CELLS, EDGE + 8, LANES), jnp.float32)],
        compiler_params=limit,
    )(far_got, edges, near_sums, lanes)
    field = pl.pallas_call(
        merge_kernel,
        out_shape=jax.ShapeDtypeStruct((1, 8, EDGE, EDGE * EDGE), jnp.float32),
        in_specs=[VMEM, VMEM],
        out_specs=VMEM,
        compiler_params=limit,
    )(near_planes, far_planes)
    sums = sums + moved(sums, beside(0, 1))
    bit = 1
    while bit < chips:
        sums = sums + moved(sums, beside(bit, 1))
        bit *= 2
    cells = start_field.size * chips * sizes[2]
    increments = jnp.sqrt(jnp.sum(sums, axis=1) / cells + 1e-06)
    return (field, increments[:, None])


def solution(mesh):
    placed = (P(("slab", "curve", "sub"), None, None), P(("slab", "curve", "sub"), None))
    return jax.shard_map(
        shards,
        mesh=mesh,
        in_specs=placed,
        out_specs=(P("node", ("slab", "curve", "sub"), None, None), P("slab", "node")),
        check_vma=False,
    )
```

time: 130 us -> 17.6 us (0.14)
  local copies, waits for them, and re-layouts: 36.9 us -> 1.58 us
  starting transfers between devices: 41.7 us -> 7.12 us
  blocking collectives: 28.2 us -> 0 us
  waiting for transfers between devices: 13.4 us -> 3.09 us
  other arithmetic: 5.1 us -> 0.65 us
  Pallas kernels: 0 us -> 4.36 us
  between operations: 3.89 us -> 0.66 us
    ppermute x16 -> x5, starting transfers between devices: 41.7 us -> 7.12 us  [moved(): return lax.ppermute(value, axes, pairs_over(sizes, partner))]
    psum x1 -> x0, blocking collectives: 16.2 us -> none  [shards(): norm_rows.append(lax.psum(local_square, ('curve', 'sub')))]
    all_gather x2 -> x0, blocking collectives: 12 us -> none  [shards(): shard_rows = lax.all_gather(forces[None], 'node', axis=0, tiled=True)]
    ppermute x16 -> x5, waiting for transfers between devices: 13.4 us -> 3.09 us  [moved(): return lax.ppermute(value, axes, pairs_over(sizes, partner))]
    slice x84 -> x0, local copies, waits for them, and re-layouts: 8.68 us -> none  [the longest x15 2.85 us: face_stack(): block_field[:, :, edge_cells - 1::edge_cells].reshape(block_count, -1)]
    reshape x24 -> x0, local copies, waits for them, and re-layouts: 7.1 us -> none  [the longest x8 3.52 us: assemble(): jnp.repeat(ghost_faces[:, 5].reshape(block_count, edge_cells, edge_cells)...]
    another operation x112 -> x0, local copies, waits for them, and re-layouts: 6.26 us -> none  [the longest x48 2.98 us: face_stack(): return jnp.stack([low_x, high_x, low_y, high_y, low_z, high_z], axis=1)]
    broadcast_in_dim x17 -> x0, local copies, waits for them, and re-layouts: 5.41 us -> none  [the longest x8 2.67 us: assemble(): jnp.repeat(ghost_faces[:, 4].reshape(block_count, edge_cells, edge_cells)...]
  transfers between devices with their start and end apart: 16 -> 5, of which waited for: 7 -> 3; matrix products, arithmetic and copies ran while one was open for 2% -> 0% of each run, Pallas kernels for 0% -> 16%
where the time goes in v2:
time: 17.6 us; the launch traced here: 17.5 us
  starting transfers between devices  7.12 us (40%)
  Pallas kernels  4.36 us (25%)
  waiting for transfers between devices  3.09 us (18%)
  local copies, waits for them, and re-layouts  1.58 us (9%)
  between operations  0.66 us (4%)
  other arithmetic  0.65 us (4%)
    ppermute x5, starting transfers between devices, moved(): return lax.ppermute(value, axes, pairs_over(sizes, partner))  7.12 us
    ppermute x5, waiting for transfers between devices, moved(): return lax.ppermute(value, axes, pairs_over(sizes, partner))  3.09 us
    pallas_call x1, Pallas kernels, shards(): pl.pallas_call(functools.partial(near_kernel, scheme), out_shape=[jax.Sha...  1.91 us
    unnamed x4, local copies, waits for them, and re-layouts  1.58 us
    pallas_call x1, Pallas kernels, shards(): pl.pallas_call(functools.partial(far_kernel, scheme), out_shape=[planes,...  1.44 us
    pallas_call x1, Pallas kernels, shards(): pl.pallas_call(merge_kernel, out_shape=jax.ShapeDtypeStruct((1, 8, EDGE,...  0.96 us
    sqrt x1, other arithmetic, shards(): increments = jnp.sqrt(jnp.sum(sums, axis=1) / cells + 1e-06)  0.53 us
  transfers between devices with their start and end apart: 5, of which 3 were waited for; matrix products, arithmetic and copies ran while one was open for 0% of the time, Pallas kernels for 16%

profile of v2, /device:TPU:0, one launch (start us, length us, event | category | flops | bytes accessed | tf_op | source)
XLA Modules:
  0.0 17.5 jit_solution(7542061602606736351)
XLA Ops:
  0.6 0.0 copy-start
  0.6 0.9 %copy-done = f32[8,16,256]{2,1,0:T(8,128)S(1)} copy-done((f32[8,16,256]{2,1,0:T(8,128)S(1)}, f32[8,16,256]{2,1,0:T(8,128)}, u32[]{:S(2)}) %copy-start) | copy-done | bytes 131096
  1.6 0.5 %collective-permute-start = (f32[8,8,256]{2,1,0:T(8,128)S(1)}, f32[8,8,256]{2,1,0:T(8,128)S(1)}, u32[]{:S(2)}, u32[]{:S(2)}) collective-permute-start(f32[8,8,256]{2,1,0:T(8,128)S(1)} %get-tuple-element.10.chip_half), channel_id=1, source_target_pairs={{0,1},{1,0},{2,3},{3,2},{4,5},{5,4},{6,7},{7,6},{8,9},{9,8},{10,11... | collective-permute-start | bytes 196616 | tf_op jit(solution)/shard_map/ppermute | solution.py:465
  2.1 2.6 %collective-permute-start.1 = (f32[8,8,256]{2,1,0:T(8,128)S(1)}, f32[8,8,256]{2,1,0:T(8,128)S(1)}, u32[]{:S(2)}, u32[]{:S(2)}) collective-permute-start(f32[8,8,256]{2,1,0:T(8,128)S(1)} %get-tuple-element.11.far_half), channel_id=1, source_target_pairs={{0,2},{1,4},{2,0},{3,6},{4,1},{5,8},{6,3},{7,10},{8,5},{9,12},{10,... | collective-permute-start | bytes 196616 | tf_op jit(solution)/shard_map/ppermute | solution.py:465
  4.7 0.0 collective-permute-done.chip_got
  4.7 0.0 copy-start.1
  4.7 0.7 %copy-done.1 = s32[8,6]{1,0:T(8,128)S(1)} copy-done((s32[8,6]{1,0:T(8,128)S(1)}, s32[8,6]{1,0:T(8,128)}, u32[]{:S(2)}) %copy-start.1) | copy-done | bytes 216
  5.4 1.9 %shard_map.42 = (f32[2,15,16,8,128]{4,3,2,1,0:T(8,128)S(1)}, f32[16,8,128]{2,1,0:T(8,128)S(1)}, f32[2,8,128]{2,1,0:T(8,128)S(1)}, s32[6,8,128]{2,1,0:T(8,128)S(1)}) custom-call(f32[8,8,256]{2,1,0:T(8,128)S(1)} %get-tuple-element.10.chip_half, f32[8,8,256]{2,1,0:T(8,128)S(1)} %get-tuple-element.11.far_half, f32[8,8,256]{2,1,0:T(8,128)S(1)} %collective-permute-done.chip_got, ...), custom_call_target="tpu_custom_call" | custom-call | flops 8000000 | bytes 2000000 | tf_op jit(solution)/shard_map/pallas_call | solution.py:477
  7.3 0.0 collective-permute-done.1.far_got
  7.3 1.4 %shard_map.43 = (f32[16,8,128]{2,1,0:T(8,128)S(1)}, f32[2,128]{1,0:T(2,128)S(1)}) custom-call(f32[8,8,256]{2,1,0:T(8,128)S(1)} %collective-permute-done.1.far_got, f32[2,15,16,8,128]{4,3,2,1,0:T(8,128)S(1)} %get-tuple-element.13.edges, f32[2,8,128]{2,1,0:T(8,128)S(1)} %get-tuple-element.14.near_sums, s32[6,8,128]{2,1,0:T(8,128)S(1)} %get-tuple-element.15.lanes), custom_call_target="tpu_custom_call" | custom-call | tf_op jit(solution)/shard_map/pallas_call | solution.py:491
  8.7 0.3 %collective-permute-start.2 = (f32[2,128]{1,0:T(2,128)S(1)}, f32[2,128]{1,0:T(2,128)S(1)}, u32[]{:S(2)}, u32[]{:S(2)}) collective-permute-start(f32[2,128]{1,0:T(2,128)S(1)} %get-tuple-element.17), channel_id=1, source_target_pairs={{0,1},{1,0},{2,3},{3,2},{4,5},{5,4},{6,7},{7,6},{8,9},{9,8},{10,11... | collective-permute-start | bytes 3080 | tf_op jit(solution)/shard_map/ppermute | solution.py:465
  9.0 0.9 %collective-permute-done.2 = f32[2,128]{1,0:T(2,128)S(1)} collective-permute-done((f32[2,128]{1,0:T(2,128)S(1)}, f32[2,128]{1,0:T(2,128)S(1)}, u32[]{:S(2)}, u32[]{:S(2)}) %collective-permute-start.2) | collective-permute-done | bytes 1056 | tf_op jit(solution)/shard_map/ppermute | solution.py:465
  9.9 1.4 %collective-permute-start.3 = (f32[2,128]{1,0:T(2,128)S(1)}, f32[2,128]{1,0:T(2,128)S(1)}, u32[]{:S(2)}, u32[]{:S(2)}) collective-permute-start(f32[2,128]{1,0:T(2,128)S(1)} %add.20), channel_id=1, source_target_pairs={{0,5},{1,4},{2,7},{3,6},{4,1},{5,0},{6,3},{7,2},{8,13},{9,12},{10,... | collective-permute-start | bytes 3080 | tf_op jit(solution)/shard_map/ppermute | solution.py:465
  11.3 1.6 %collective-permute-done.3 = f32[2,128]{1,0:T(2,128)S(1)} collective-permute-done((f32[2,128]{1,0:T(2,128)S(1)}, f32[2,128]{1,0:T(2,128)S(1)}, u32[]{:S(2)}, u32[]{:S(2)}) %collective-permute-start.3) | collective-permute-done | bytes 1056 | tf_op jit(solution)/shard_map/ppermute | solution.py:465
  12.9 2.4 %collective-permute-start.4 = (f32[2,128]{1,0:T(2,128)S(1)}, f32[2,128]{1,0:T(2,128)S(1)}, u32[]{:S(2)}, u32[]{:S(2)}) collective-permute-start(f32[2,128]{1,0:T(2,128)S(1)} %add.21), channel_id=1, source_target_pairs={{0,9},{1,8},{2,11},{3,10},{4,13},{5,12},{6,15},{7,14},{8,1},{9,0},... | collective-permute-start | bytes 3080 | tf_op jit(solution)/shard_map/ppermute | solution.py:465
  15.3 1.0 %shard_map.44 = f32[1,8,16,256]{3,2,1,0:T(8,128)} custom-call(f32[16,8,128]{2,1,0:T(8,128)S(1)} %get-tuple-element.12.near, f32[16,8,128]{2,1,0:T(8,128)S(1)} %get-tuple-element.16.far), custom_call_target="tpu_custom_call" | custom-call | tf_op jit(solution)/shard_map/pallas_call | solution.py:499
  16.3 0.5 %collective-permute-done.4 = f32[2,128]{1,0:T(2,128)S(1)} collective-permute-done((f32[2,128]{1,0:T(2,128)S(1)}, f32[2,128]{1,0:T(2,128)S(1)}, u32[]{:S(2)}, u32[]{:S(2)}) %collective-permute-start.4) | collective-permute-done | bytes 1056 | tf_op jit(solution)/shard_map/ppermute | solution.py:465
  16.8 0.1 add_reduce_fusion
  16.9 0.5 %sqrt_bitcast_fusion = f32[2,1]{0,1:T(1,128)} fusion(f32[2]{0:T(128)S(1)} %add_reduce_fusion), kind=kLoop, calls=%fused_computation.1 | loop fusion | flops 4 | bytes 16 | tf_op jit(solution)/shard_map/sqrt | solution.py:512
  (3 shorter events, 0.0 us)
Async XLA Ops:
  0.6 0.9 %copy-start = (f32[8,16,256]{2,1,0:T(8,128)S(1)}, f32[8,16,256]{2,1,0:T(8,128)}, u32[]{:S(2)}) copy-start(f32[8,16,256]{2,1,0:T(8,128)} %field.1) | copy-start | bytes 393220
  1.6 3.1 %collective-permute-start = (f32[8,8,256]{2,1,0:T(8,128)S(1)}, f32[8,8,256]{2,1,0:T(8,128)S(1)}, u32[]{:S(2)}, u32[]{:S(2)}) collective-permute-start(f32[8,8,256]{2,1,0:T(8,128)S(1)} %get-tuple-element.10.chip_half), channel_id=1, source_target_pairs={{0,1},{1,0},{2,3},{3,2},{4,5},{5,4},{6,7},{7,6},{8,9},{9,8},{10,11... | collective-permute-start | bytes 196616 | tf_op jit(solution)/shard_map/ppermute | solution.py:465
  2.1 5.2 %collective-permute-start.1 = (f32[8,8,256]{2,1,0:T(8,128)S(1)}, f32[8,8,256]{2,1,0:T(8,128)S(1)}, u32[]{:S(2)}, u32[]{:S(2)}) collective-permute-start(f32[8,8,256]{2,1,0:T(8,128)S(1)} %get-tuple-element.11.far_half), channel_id=1, source_target_pairs={{0,2},{1,4},{2,0},{3,6},{4,1},{5,8},{6,3},{7,10},{8,5},{9,12},{10,... | collective-permute-start | bytes 196616 | tf_op jit(solution)/shard_map/ppermute | solution.py:465
  4.7 0.7 %copy-start.1 = (s32[8,6]{1,0:T(8,128)S(1)}, s32[8,6]{1,0:T(8,128)}, u32[]{:S(2)}) copy-start(s32[8,6]{1,0:T(8,128)} %table.1) | copy-start | bytes 580
  8.7 1.2 %collective-permute-start.2 = (f32[2,128]{1,0:T(2,128)S(1)}, f32[2,128]{1,0:T(2,128)S(1)}, u32[]{:S(2)}, u32[]{:S(2)}) collective-permute-start(f32[2,128]{1,0:T(2,128)S(1)} %get-tuple-element.17), channel_id=1, source_target_pairs={{0,1},{1,0},{2,3},{3,2},{4,5},{5,4},{6,7},{7,6},{8,9},{9,8},{10,11... | collective-permute-start | bytes 3080 | tf_op jit(solution)/shard_map/ppermute | solution.py:465
  9.9 3.0 %collective-permute-start.3 = (f32[2,128]{1,0:T(2,128)S(1)}, f32[2,128]{1,0:T(2,128)S(1)}, u32[]{:S(2)}, u32[]{:S(2)}) collective-permute-start(f32[2,128]{1,0:T(2,128)S(1)} %add.20), channel_id=1, source_target_pairs={{0,5},{1,4},{2,7},{3,6},{4,1},{5,0},{6,3},{7,2},{8,13},{9,12},{10,... | collective-permute-start | bytes 3080 | tf_op jit(solution)/shard_map/ppermute | solution.py:465
  12.9 3.9 %collective-permute-start.4 = (f32[2,128]{1,0:T(2,128)S(1)}, f32[2,128]{1,0:T(2,128)S(1)}, u32[]{:S(2)}, u32[]{:S(2)}) collective-permute-start(f32[2,128]{1,0:T(2,128)S(1)} %add.21), channel_id=1, source_target_pairs={{0,9},{1,8},{2,11},{3,10},{4,13},{5,12},{6,15},{7,14},{8,1},{9,0},... | collective-permute-start | bytes 3080 | tf_op jit(solution)/shard_map/ppermute | solution.py:465

commit v3 on v2

--- a/solution.py
+++ b/solution.py
@@ -106,6 +106,39 @@
         store(cell_of(index), value)
 
 
+def spread_to(source, route, store):
+    lane = lax.broadcasted_iota(jnp.int32, (8, LANES), 1)
+    values = [source[index & 7, :, (index >> 3) * LANES : (index >> 3) * LANES + LANES] for index in range(CELLS)]
+    for stage, origin in ((0, None), (2, route)):
+        (bit_a, lane_a), (bit_b, lane_b) = SWAPS[stage : stage + 2]
+        spot = lane if origin is None else origin
+        high_a = (spot >> lane_a) & 1 == 1
+        high_b = (spot >> lane_b) & 1 == 1
+        shifts = {}
+
+        def moved_by(value, step_a, step_b):
+            shift = step_a * (1 << lane_a) + step_b * (1 << lane_b)
+            if origin is None:
+                return value if shift == 0 else pltpu.roll(value, -shift % LANES, 1)
+            if shift not in shifts:
+                shifts[shift] = (origin + shift) & (LANES - 1)
+            return picked(value, shifts[shift])
+
+        out = []
+        for index in range(CELLS):
+            base = index & ~(bit_a | bit_b)
+            own_a, own_b = int(index & bit_a != 0), int(index & bit_b != 0)
+            parts = [
+                [moved_by(values[base | p * bit_a | q * bit_b], own_a - p, own_b - q) for q in range(2)]
+                for p in range(2)
+            ]
+            rows = [jnp.where(high_b, part[1], part[0]) for part in parts]
+            out.append(jnp.where(high_a, rows[1], rows[0]))
+        values = out
+    for index, value in enumerate(values):
+        store(cell_of(index), value)
+
+
 def lane_of(slot, outer_j, outer_k):
     return (
         (outer_j & 1) << 6
@@ -260,7 +293,7 @@
         return self.own(node, self.stiffness) * self.own(node, self.scales)
 
 
-def near_kernel(scheme, chip_half, far_half, chip_got, table, edges, planes, sums, lanes, state):
+def near_kernel(scheme, chip_half, far_half, chip_got, table, edges, mirror, planes, sums, lanes, state):
     sub = lax.axis_index("sub")
     node = lax.axis_index("node")
     nodes = scheme.nodes
@@ -268,14 +301,15 @@
     for index, route in enumerate(routes):
         lanes[index] = route
     faces = face_routes(routes)
+    below, above = slice(0, 8), slice(16, 24)
     low_half = pl.ds(pl.multiple_of(sub * 16, 8), 8)
     chip_half_rows = pl.ds(8, 8)
     high_half = pl.ds(pl.multiple_of(16 - sub * 16, 8), 8)
 
     def store_far(cell, value):
         state[0, cell, low_half] = value
-        edges[0, 0, cell] = value
-        edges[1, 0, cell] = value
+        edges[0, cell, above] = value
+        edges[0, cell, below] = value
 
     def store_chip(cell, value):
         state[0, cell, chip_half_rows] = value
@@ -286,6 +320,8 @@
     spread(far_half, store_far)
     spread(chip_half, store_chip)
     spread(chip_got, store_got)
+    for row in range(8):
+        mirror[:, 7 - row : 8 - row, :] = edges[0, :, row : row + 1, :]
 
     span = EDGE + 8
 
@@ -298,9 +334,9 @@
     def keep(index, level, start, cell, value):
         state[index, cell, pl.ds(start, 8)] = value
         if start == level:
-            edges[0, index, cell] = value
+            edges[index, cell, above] = value
         if start == span - 8 - level:
-            edges[1, index, cell] = value
+            edges[index, cell, below] = value
 
     for start in starts(1):
         for cell, value, total in around_at(state.at[0], start, 1, faces):
@@ -345,29 +381,28 @@
     sums[1] = second_square
 
 
-def far_kernel(scheme, far_got, edges, near_sums, lanes, planes, sums, state):
+def far_kernel(scheme, far_got, edges, mirror, near_sums, lanes, planes, sums, state):
     sub = lax.axis_index("sub")
+    for side in range(2):
+
+        @pl.when(sub == side)
+        def _():
+            far_side(scheme, side, far_got, mirror, near_sums, lanes, planes, sums, state)
+
+
+def far_side(scheme, side, far_got, mirror, near_sums, lanes, planes, sums, state):
     curve = lax.axis_index("curve")
     node = lax.axis_index("node")
     nodes = scheme.nodes
     faces = face_routes([lanes[index] for index in range(4)])
-    toward = 1 - 2 * sub
-    at_end = jnp.where(sub == 0, curve == 0, curve == lax.axis_size("curve") - 1)
-    beside = pl.ds(pl.multiple_of(8 + 8 * toward, 8), 8)
+    toward = 1 - 2 * side
+    at_end = curve == (0 if side == 0 else lax.axis_size("curve") - 1)
     new = pl.ds(8, 8)
-    for index in range(scheme.count):
-        for cell in range(CELLS):
-            state[index, cell, beside] = edges[sub, index, cell]
 
     def store_far(cell, value):
-        state[0, cell, new] = picked(value, lanes[5])
-
-    spread(far_got, store_far)
-
-    @pl.when(at_end)
-    def _():
-        for row in range(8):
-            state[0, :, 15 - row : 16 - row, :] = edges[sub, 0, :, row : row + 1, :]
+        state[0, cell, new] = jnp.where(at_end, mirror[cell], value)
+
+    spread_to(far_got, lanes[5], store_far)
 
     def shifted(levels):
         return pl.ds(8 + toward * levels, 8)
@@ -414,19 +449,24 @@
             right = state[scheme.right(1), cell, shifted(level - JACOBI - 1)]
             pending.append((scheme.field(level), cell, right + factor * total))
         write(pending)
-    first_square = near_sums[0]
-    second_square = near_sums[1]
     level = 2 * JACOBI
+    first_squares, second_squares = [near_sums[0]], [near_sums[1]]
     for cell, value, total in ring(scheme.field(level - 1)):
         update = state[scheme.right(1), cell, shifted(JACOBI - 1)] + factor * total
         planes[cell] = update
         earlier = state[scheme.field(JACOBI) + node, cell, shifted(JACOBI)]
         change = update - earlier
-        second_square = second_square + change * change
+        second_squares.append(change * change)
         change = earlier - state[0, cell, shifted(level)]
-        first_square = first_square + change * change
-    sums[0:1, :] = jnp.sum(first_square, axis=0, keepdims=True)
-    sums[1:2, :] = jnp.sum(second_square, axis=0, keepdims=True)
+        first_squares.append(change * change)
+    sums[0] = added(first_squares)
+    sums[1] = added(second_squares)
+
+
+def added(terms):
+    while len(terms) > 1:
+        terms = [sum(terms[place + 1 : place + 2], terms[place]) for place in range(0, len(terms), 2)]
+    return terms[0]
 
 
 def pairs_over(sizes, partner):
@@ -474,28 +514,30 @@
     )(start_field)
     far_got = moved(far_half, across)
     chip_got = moved(chip_half, beside(0, 1))
-    edges, near_planes, near_sums, lanes = pl.pallas_call(
+    shared = jax.ShapeDtypeStruct((scheme.count, CELLS, EDGE + 8, LANES), jnp.float32)
+    edges, mirror, near_planes, near_sums, lanes = pl.pallas_call(
         functools.partial(near_kernel, scheme),
         out_shape=[
-            jax.ShapeDtypeStruct((2, scheme.count, CELLS, 8, LANES), jnp.float32),
+            shared,
+            planes,
             planes,
             jax.ShapeDtypeStruct((2, 8, LANES), jnp.float32),
             jax.ShapeDtypeStruct((6, 8, LANES), jnp.int32),
         ],
         in_specs=[VMEM] * 4,
-        out_specs=[VMEM] * 4,
-        scratch_shapes=[pltpu.VMEM((scheme.count, CELLS, EDGE + 8, LANES), jnp.float32)],
+        out_specs=[VMEM] * 5,
+        scratch_shapes=[pltpu.VMEM(shared.shape, jnp.float32)],
         compiler_params=limit,
         cost_estimate=pl.CostEstimate(flops=8_000_000, bytes_accessed=2_000_000, transcendentals=0),
     )(chip_half, far_half, chip_got, neighbours)
-    far_planes, sums = pl.pallas_call(
+    far_planes, sums, _ = pl.pallas_call(
         functools.partial(far_kernel, scheme),
-        out_shape=[planes, jax.ShapeDtypeStruct((2, LANES), jnp.float32)],
-        in_specs=[VMEM] * 4,
-        out_specs=[VMEM, VMEM],
-        scratch_shapes=[pltpu.VMEM((scheme.count, CELLS, EDGE + 8, LANES), jnp.float32)],
+        out_shape=[planes, jax.ShapeDtypeStruct((2, 8, LANES), jnp.float32), shared],
+        in_specs=[VMEM] * 5,
+        out_specs=[VMEM] * 3,
+        input_output_aliases={1: 2},
         compiler_params=limit,
-    )(far_got, edges, near_sums, lanes)
+    )(far_got, edges, mirror, near_sums, lanes)
     field = pl.pallas_call(
         merge_kernel,
         out_shape=jax.ShapeDtypeStruct((1, 8, EDGE, EDGE * EDGE), jnp.float32),
@@ -509,7 +551,7 @@
         sums = sums + moved(sums, beside(bit, 1))
         bit *= 2
     cells = start_field.size * chips * sizes[2]
-    increments = jnp.sqrt(jnp.sum(sums, axis=1) / cells + 1e-06)
+    increments = jnp.sqrt(jnp.sum(sums, axis=(1, 2)) / cells + 1e-06)
     return (field, increments[:, None])
 
 

time: 17.6 us -> 17.7 us (level)
  waiting for transfers between devices: 3.09 us -> 3.28 us
  Pallas kernels: 4.36 us -> 4.18 us
    ppermute x5, waiting for transfers between devices: 3.09 us -> 3.28 us  [moved(): return lax.ppermute(value, axes, pairs_over(sizes, partner))]
    pallas_call x1, Pallas kernels: 1.44 us -> 1.26 us  [shards(): pl.pallas_call(functools.partial(far_kernel, scheme), out_shape=[planes,...]
where the time goes in v3:
time: 17.7 us; the launch traced here: 17.5 us
  starting transfers between devices  7.13 us (40%)
  Pallas kernels  4.18 us (24%)
  waiting for transfers between devices  3.28 us (19%)
  local copies, waits for them, and re-layouts  1.58 us (9%)
  between operations  0.67 us (4%)
  other arithmetic  0.63 us (4%)
    ppermute x5, starting transfers between devices, moved(): return lax.ppermute(value, axes, pairs_over(sizes, partner))  7.13 us
    ppermute x5, waiting for transfers between devices, moved(): return lax.ppermute(value, axes, pairs_over(sizes, partner))  3.28 us
    pallas_call x1, Pallas kernels, shards(): pl.pallas_call(functools.partial(near_kernel, scheme), out_shape=[shared,...  1.91 us
    unnamed x4, local copies, waits for them, and re-layouts  1.58 us
    pallas_call x1, Pallas kernels, shards(): pl.pallas_call(functools.partial(far_kernel, scheme), out_shape=[planes,...  1.26 us
    pallas_call x1, Pallas kernels, shards(): pl.pallas_call(merge_kernel, out_shape=jax.ShapeDtypeStruct((1, 8, EDGE,...  0.96 us
    sqrt x1, other arithmetic, shards(): increments = jnp.sqrt(jnp.sum(sums, axis=(1, 2)) / cells + 1e-06)  0.53 us
  transfers between devices with their start and end apart: 5, of which 3 were waited for; matrix products, arithmetic and copies ran while one was open for 0% of the time, Pallas kernels for 16%

profile of v3, /device:TPU:0, one launch (start us, length us, event | category | flops | bytes accessed | tf_op | source)
XLA Modules:
  0.0 17.5 jit_solution(4758316549157105541)
XLA Ops:
  0.6 0.0 copy-start
  0.6 0.9 %copy-done = f32[8,16,256]{2,1,0:T(8,128)S(1)} copy-done((f32[8,16,256]{2,1,0:T(8,128)S(1)}, f32[8,16,256]{2,1,0:T(8,128)}, u32[]{:S(2)}) %copy-start) | copy-done | bytes 131096
  1.6 0.5 %collective-permute-start = (f32[8,8,256]{2,1,0:T(8,128)S(1)}, f32[8,8,256]{2,1,0:T(8,128)S(1)}, u32[]{:S(2)}, u32[]{:S(2)}) collective-permute-start(f32[8,8,256]{2,1,0:T(8,128)S(1)} %get-tuple-element.11.chip_half), channel_id=1, source_target_pairs={{0,1},{1,0},{2,3},{3,2},{4,5},{5,4},{6,7},{7,6},{8,9},{9,8},{10,11... | collective-permute-start | bytes 196616 | tf_op jit(solution)/shard_map/ppermute | solution.py:505
  2.1 2.6 %collective-permute-start.1 = (f32[8,8,256]{2,1,0:T(8,128)S(1)}, f32[8,8,256]{2,1,0:T(8,128)S(1)}, u32[]{:S(2)}, u32[]{:S(2)}) collective-permute-start(f32[8,8,256]{2,1,0:T(8,128)S(1)} %get-tuple-element.12.far_half), channel_id=1, source_target_pairs={{0,2},{1,4},{2,0},{3,6},{4,1},{5,8},{6,3},{7,10},{8,5},{9,12},{10,... | collective-permute-start | bytes 196616 | tf_op jit(solution)/shard_map/ppermute | solution.py:505
  4.7 0.0 collective-permute-done.chip_got
  4.7 0.0 copy-start.1
  4.7 0.7 %copy-done.1 = s32[8,6]{1,0:T(8,128)S(1)} copy-done((s32[8,6]{1,0:T(8,128)S(1)}, s32[8,6]{1,0:T(8,128)}, u32[]{:S(2)}) %copy-start.1) | copy-done | bytes 216
  5.4 1.9 %shard_map.42 = (f32[15,16,24,128]{3,2,1,0:T(8,128)S(1)}, f32[16,8,128]{2,1,0:T(8,128)S(1)}, f32[16,8,128]{2,1,0:T(8,128)S(1)}, f32[2,8,128]{2,1,0:T(8,128)S(1)}, s32[6,8,128]{2,1,0:T(8,128)S(1)}) custom-call(f32[8,8,256]{2,1,0:T(8,128)S(1)} %get-tuple-element.11.chip_half, f32[8,8,256]{2,1,0:T(8,128)S(1)} %get-tuple-element.12.far_half, ...), custom_call_target="tpu_custom_call" | custom-call | flops 8000000 | bytes 2000000 | tf_op jit(solution)/shard_map/pallas_call | solution.py:518
  7.3 0.0 collective-permute-done.1.far_got
  7.3 1.3 %shard_map.43 = (f32[16,8,128]{2,1,0:T(8,128)S(1)}, f32[2,8,128]{2,1,0:T(8,128)S(1)}, f32[15,16,24,128]{3,2,1,0:T(8,128)S(1)}) custom-call(f32[8,8,256]{2,1,0:T(8,128)S(1)} %collective-permute-done.1.far_got, f32[15,16,24,128]{3,2,1,0:T(8,128)S(1)} %get-tuple-element.14.edges, ...), custom_call_target="tpu_custom_call", output_to_operand_aliasing={{2}: (1, {})} | custom-call | tf_op jit(solution)/shard_map/pallas_call | solution.py:533
  8.6 0.3 %collective-permute-start.2 = (f32[2,8,128]{2,1,0:T(8,128)S(1)}, f32[2,8,128]{2,1,0:T(8,128)S(1)}, u32[]{:S(2)}, u32[]{:S(2)}) collective-permute-start(f32[2,8,128]{2,1,0:T(8,128)S(1)} %get-tuple-element.19), channel_id=1, source_target_pairs={{0,1},{1,0},{2,3},{3,2},{4,5},{5,4},{6,7},{7,6},{8,9},{9,8},{10,11... | collective-permute-start | bytes 24584 | tf_op jit(solution)/shard_map/ppermute | solution.py:505
  8.8 1.0 %collective-permute-done.2 = f32[2,8,128]{2,1,0:T(8,128)S(1)} collective-permute-done((f32[2,8,128]{2,1,0:T(8,128)S(1)}, f32[2,8,128]{2,1,0:T(8,128)S(1)}, u32[]{:S(2)}, u32[]{:S(2)}) %collective-permute-start.2) | collective-permute-done | bytes 8224 | tf_op jit(solution)/shard_map/ppermute | solution.py:505
  9.8 1.4 %collective-permute-start.3 = (f32[2,8,128]{2,1,0:T(8,128)S(1)}, f32[2,8,128]{2,1,0:T(8,128)S(1)}, u32[]{:S(2)}, u32[]{:S(2)}) collective-permute-start(f32[2,8,128]{2,1,0:T(8,128)S(1)} %add.20), channel_id=1, source_target_pairs={{0,5},{1,4},{2,7},{3,6},{4,1},{5,0},{6,3},{7,2},{8,13},{9,12},{10,... | collective-permute-start | bytes 24584 | tf_op jit(solution)/shard_map/ppermute | solution.py:505
  11.2 1.7 %collective-permute-done.3 = f32[2,8,128]{2,1,0:T(8,128)S(1)} collective-permute-done((f32[2,8,128]{2,1,0:T(8,128)S(1)}, f32[2,8,128]{2,1,0:T(8,128)S(1)}, u32[]{:S(2)}, u32[]{:S(2)}) %collective-permute-start.3) | collective-permute-done | bytes 8224 | tf_op jit(solution)/shard_map/ppermute | solution.py:505
  12.9 2.4 %collective-permute-start.4 = (f32[2,8,128]{2,1,0:T(8,128)S(1)}, f32[2,8,128]{2,1,0:T(8,128)S(1)}, u32[]{:S(2)}, u32[]{:S(2)}) collective-permute-start(f32[2,8,128]{2,1,0:T(8,128)S(1)} %add.21), channel_id=1, source_target_pairs={{0,9},{1,8},{2,11},{3,10},{4,13},{5,12},{6,15},{7,14},{8,1},{9,0},... | collective-permute-start | bytes 24584 | tf_op jit(solution)/shard_map/ppermute | solution.py:505
  15.3 1.0 %shard_map.44 = f32[1,8,16,256]{3,2,1,0:T(8,128)} custom-call(f32[16,8,128]{2,1,0:T(8,128)S(1)} %get-tuple-element.13.near, f32[16,8,128]{2,1,0:T(8,128)S(1)} %get-tuple-element.18.far), custom_call_target="tpu_custom_call" | custom-call | tf_op jit(solution)/shard_map/pallas_call | solution.py:541
  16.2 0.6 %collective-permute-done.4 = f32[2,8,128]{2,1,0:T(8,128)S(1)} collective-permute-done((f32[2,8,128]{2,1,0:T(8,128)S(1)}, f32[2,8,128]{2,1,0:T(8,128)S(1)}, u32[]{:S(2)}, u32[]{:S(2)}) %collective-permute-start.4) | collective-permute-done | bytes 8224 | tf_op jit(solution)/shard_map/ppermute | solution.py:505
  16.9 0.1 add_reduce_fusion
  17.0 0.5 %sqrt_bitcast_fusion = f32[2,1]{0,1:T(1,128)} fusion(f32[2]{0:T(128)S(1)} %add_reduce_fusion), kind=kLoop, calls=%fused_computation.1 | loop fusion | flops 4 | bytes 16 | tf_op jit(solution)/shard_map/sqrt | solution.py:554
  (3 shorter events, 0.0 us)
Async XLA Ops:
  0.6 0.9 %copy-start = (f32[8,16,256]{2,1,0:T(8,128)S(1)}, f32[8,16,256]{2,1,0:T(8,128)}, u32[]{:S(2)}) copy-start(f32[8,16,256]{2,1,0:T(8,128)} %field.1) | copy-start | bytes 393220
  1.6 3.1 %collective-permute-start = (f32[8,8,256]{2,1,0:T(8,128)S(1)}, f32[8,8,256]{2,1,0:T(8,128)S(1)}, u32[]{:S(2)}, u32[]{:S(2)}) collective-permute-start(f32[8,8,256]{2,1,0:T(8,128)S(1)} %get-tuple-element.11.chip_half), channel_id=1, source_target_pairs={{0,1},{1,0},{2,3},{3,2},{4,5},{5,4},{6,7},{7,6},{8,9},{9,8},{10,11... | collective-permute-start | bytes 196616 | tf_op jit(solution)/shard_map/ppermute | solution.py:505
  2.1 5.2 %collective-permute-start.1 = (f32[8,8,256]{2,1,0:T(8,128)S(1)}, f32[8,8,256]{2,1,0:T(8,128)S(1)}, u32[]{:S(2)}, u32[]{:S(2)}) collective-permute-start(f32[8,8,256]{2,1,0:T(8,128)S(1)} %get-tuple-element.12.far_half), channel_id=1, source_target_pairs={{0,2},{1,4},{2,0},{3,6},{4,1},{5,8},{6,3},{7,10},{8,5},{9,12},{10,... | collective-permute-start | bytes 196616 | tf_op jit(solution)/shard_map/ppermute | solution.py:505
  4.7 0.7 %copy-start.1 = (s32[8,6]{1,0:T(8,128)S(1)}, s32[8,6]{1,0:T(8,128)}, u32[]{:S(2)}) copy-start(s32[8,6]{1,0:T(8,128)} %table.1) | copy-start | bytes 580
  8.6 1.2 %collective-permute-start.2 = (f32[2,8,128]{2,1,0:T(8,128)S(1)}, f32[2,8,128]{2,1,0:T(8,128)S(1)}, u32[]{:S(2)}, u32[]{:S(2)}) collective-permute-start(f32[2,8,128]{2,1,0:T(8,128)S(1)} %get-tuple-element.19), channel_id=1, source_target_pairs={{0,1},{1,0},{2,3},{3,2},{4,5},{5,4},{6,7},{7,6},{8,9},{9,8},{10,11... | collective-permute-start | bytes 24584 | tf_op jit(solution)/shard_map/ppermute | solution.py:505
  9.8 3.1 %collective-permute-start.3 = (f32[2,8,128]{2,1,0:T(8,128)S(1)}, f32[2,8,128]{2,1,0:T(8,128)S(1)}, u32[]{:S(2)}, u32[]{:S(2)}) collective-permute-start(f32[2,8,128]{2,1,0:T(8,128)S(1)} %add.20), channel_id=1, source_target_pairs={{0,5},{1,4},{2,7},{3,6},{4,1},{5,0},{6,3},{7,2},{8,13},{9,12},{10,... | collective-permute-start | bytes 24584 | tf_op jit(solution)/shard_map/ppermute | solution.py:505
  12.9 4.0 %collective-permute-start.4 = (f32[2,8,128]{2,1,0:T(8,128)S(1)}, f32[2,8,128]{2,1,0:T(8,128)S(1)}, u32[]{:S(2)}, u32[]{:S(2)}) collective-permute-start(f32[2,8,128]{2,1,0:T(8,128)S(1)} %add.21), channel_id=1, source_target_pairs={{0,9},{1,8},{2,11},{3,10},{4,13},{5,12},{6,15},{7,14},{8,1},{9,0},... | collective-permute-start | bytes 24584 | tf_op jit(solution)/shard_map/ppermute | solution.py:505

commit v4 on v3

--- a/solution.py
+++ b/solution.py
@@ -315,11 +315,11 @@
         state[0, cell, chip_half_rows] = value
 
     def store_got(cell, value):
-        state[0, cell, high_half] = picked(value, routes[4])
+        state[0, cell, high_half] = value
 
     spread(far_half, store_far)
     spread(chip_half, store_chip)
-    spread(chip_got, store_got)
+    spread_to(chip_got, routes[4], store_got)
     for row in range(8):
         mirror[:, 7 - row : 8 - row, :] = edges[0, :, row : row + 1, :]
 
@@ -364,8 +364,7 @@
             for cell, value, total in around_at(state.at[scheme.field(level - 1)], start, 1, faces):
                 right = state[scheme.right(1), cell, pl.ds(start, 8)]
                 keep(scheme.field(level), level, start, cell, right + factor * total)
-    first_square = jnp.zeros((8, LANES), jnp.float32)
-    second_square = jnp.zeros((8, LANES), jnp.float32)
+    first_squares, second_squares = [], []
     start = 2 * JACOBI
     rows = pl.ds(start, 8)
     earlier_place = scheme.field(JACOBI) + node
@@ -374,11 +373,11 @@
         planes[cell] = update
         earlier = state[earlier_place, cell, rows]
         change = update - earlier
-        second_square = second_square + change * change
+        second_squares.append(change * change)
         change = earlier - state[0, cell, rows]
-        first_square = first_square + change * change
-    sums[0] = first_square
-    sums[1] = second_square
+        first_squares.append(change * change)
+    sums[0] = added(first_squares)
+    sums[1] = added(second_squares)
 
 
 def far_kernel(scheme, far_got, edges, mirror, near_sums, lanes, planes, sums, state):
@@ -459,8 +458,14 @@
         second_squares.append(change * change)
         change = earlier - state[0, cell, shifted(level)]
         first_squares.append(change * change)
-    sums[0] = added(first_squares)
-    sums[1] = added(second_squares)
+    sums[0:1, :] = jnp.sum(added(first_squares), axis=0, keepdims=True)
+    sums[1:2, :] = jnp.sum(added(second_squares), axis=0, keepdims=True)
+
+
+def norm_kernel(cells, sums, got, norms):
+    totals = jnp.sum(sums[...] + got[...], axis=1, keepdims=True)
+    lane = lax.broadcasted_iota(jnp.int32, (1, 2), 1)
+    norms[...] = jnp.sqrt(jnp.where(lane == 0, totals[0:1], totals[1:2]) / cells + 1e-06)
 
 
 def added(terms):
@@ -532,7 +537,7 @@
     )(chip_half, far_half, chip_got, neighbours)
     far_planes, sums, _ = pl.pallas_call(
         functools.partial(far_kernel, scheme),
-        out_shape=[planes, jax.ShapeDtypeStruct((2, 8, LANES), jnp.float32), shared],
+        out_shape=[planes, jax.ShapeDtypeStruct((2, LANES), jnp.float32), shared],
         in_specs=[VMEM] * 5,
         out_specs=[VMEM] * 3,
         input_output_aliases={1: 2},
@@ -545,14 +550,22 @@
         out_specs=VMEM,
         compiler_params=limit,
     )(near_planes, far_planes)
-    sums = sums + moved(sums, beside(0, 1))
+    rounds = [beside(0, 1)]
     bit = 1
     while bit < chips:
-        sums = sums + moved(sums, beside(bit, 1))
+        rounds.append(beside(bit, 1))
         bit *= 2
+    for partner in rounds[:-1]:
+        sums = sums + moved(sums, partner)
     cells = start_field.size * chips * sizes[2]
-    increments = jnp.sqrt(jnp.sum(sums, axis=(1, 2)) / cells + 1e-06)
-    return (field, increments[:, None])
+    increments = pl.pallas_call(
+        functools.partial(norm_kernel, np.float32(cells)),
+        out_shape=jax.ShapeDtypeStruct((1, SWEEPS), jnp.float32),
+        in_specs=[VMEM, VMEM],
+        out_specs=VMEM,
+        compiler_params=limit,
+    )(sums, moved(sums, rounds[-1]))
+    return (field, increments.T)
 
 
 def solution(mesh):

time: 17.7 us -> 17.5 us (0.989)
  Pallas kernels: 4.18 us -> 4.88 us
  other arithmetic: 0.63 us -> 0.01 us
  waiting for transfers between devices: 3.28 us -> 3.08 us
    pallas_call x0 -> x1, Pallas kernels: none -> 0.6 us  [shards(): pl.pallas_call(functools.partial(norm_kernel, np.float32(cells)), out_sha...]
    sqrt x1 -> x0, other arithmetic: 0.53 us -> none  [shards(): increments = jnp.sqrt(jnp.sum(sums, axis=(1, 2)) / cells + 1e-06)]
    ppermute x5, waiting for transfers between devices: 3.28 us -> 3.08 us  [moved(): return lax.ppermute(value, axes, pairs_over(sizes, partner))]
  transfers between devices with their start and end apart: 5 -> 5, of which waited for: 3 -> 3; matrix products, arithmetic and copies ran while one was open for 0% -> 0% of each run, Pallas kernels for 16% -> 17%
where the time goes in v4:
time: 17.5 us; the launch traced here: 17.4 us
  starting transfers between devices  7.14 us (41%)
  Pallas kernels  4.88 us (28%)
  waiting for transfers between devices  3.08 us (18%)
  local copies, waits for them, and re-layouts  1.58 us (9%)
  between operations  0.67 us (4%)
    ppermute x5, starting transfers between devices, moved(): return lax.ppermute(value, axes, pairs_over(sizes, partner))  7.14 us
    ppermute x5, waiting for transfers between devices, moved(): return lax.ppermute(value, axes, pairs_over(sizes, partner))  3.08 us
    pallas_call x1, Pallas kernels, shards(): pl.pallas_call(functools.partial(near_kernel, scheme), out_shape=[shared,...  1.95 us
    unnamed x4, local copies, waits for them, and re-layouts  1.58 us
    pallas_call x1, Pallas kernels, shards(): pl.pallas_call(functools.partial(far_kernel, scheme), out_shape=[planes,...  1.32 us
    pallas_call x1, Pallas kernels, shards(): pl.pallas_call(merge_kernel, out_shape=jax.ShapeDtypeStruct((1, 8, EDGE,...  0.96 us
    pallas_call x1, Pallas kernels, shards(): pl.pallas_call(functools.partial(norm_kernel, np.float32(cells)), out_sha...  0.6 us
  transfers between devices with their start and end apart: 5, of which 3 were waited for; matrix products, arithmetic and copies ran while one was open for 0% of the time, Pallas kernels for 17%

profile of v4, /device:TPU:0, one launch (start us, length us, event | category | flops | bytes accessed | tf_op | source)
XLA Modules:
  0.0 17.4 jit_solution(6326889160522392293)
XLA Ops:
  0.6 0.0 copy-start
  0.6 0.9 %copy-done = f32[8,16,256]{2,1,0:T(8,128)S(1)} copy-done((f32[8,16,256]{2,1,0:T(8,128)S(1)}, f32[8,16,256]{2,1,0:T(8,128)}, u32[]{:S(2)}) %copy-start) | copy-done | bytes 131096
  1.6 0.5 %collective-permute-start = (f32[8,8,256]{2,1,0:T(8,128)S(1)}, f32[8,8,256]{2,1,0:T(8,128)S(1)}, u32[]{:S(2)}, u32[]{:S(2)}) collective-permute-start(f32[8,8,256]{2,1,0:T(8,128)S(1)} %get-tuple-element.11.chip_half), channel_id=1, source_target_pairs={{0,1},{1,0},{2,3},{3,2},{4,5},{5,4},{6,7},{7,6},{8,9},{9,8},{10,11... | collective-permute-start | bytes 196616 | tf_op jit(solution)/shard_map/ppermute | solution.py:510
  2.1 2.6 %collective-permute-start.1 = (f32[8,8,256]{2,1,0:T(8,128)S(1)}, f32[8,8,256]{2,1,0:T(8,128)S(1)}, u32[]{:S(2)}, u32[]{:S(2)}) collective-permute-start(f32[8,8,256]{2,1,0:T(8,128)S(1)} %get-tuple-element.12.far_half), channel_id=1, source_target_pairs={{0,2},{1,4},{2,0},{3,6},{4,1},{5,8},{6,3},{7,10},{8,5},{9,12},{10,... | collective-permute-start | bytes 196616 | tf_op jit(solution)/shard_map/ppermute | solution.py:510
  4.7 0.0 collective-permute-done.chip_got
  4.7 0.0 copy-start.1
  4.7 0.7 %copy-done.1 = s32[8,6]{1,0:T(8,128)S(1)} copy-done((s32[8,6]{1,0:T(8,128)S(1)}, s32[8,6]{1,0:T(8,128)}, u32[]{:S(2)}) %copy-start.1) | copy-done | bytes 216
  5.4 2.0 %shard_map.42 = (f32[15,16,24,128]{3,2,1,0:T(8,128)S(1)}, f32[16,8,128]{2,1,0:T(8,128)S(1)}, f32[16,8,128]{2,1,0:T(8,128)S(1)}, f32[2,8,128]{2,1,0:T(8,128)S(1)}, s32[6,8,128]{2,1,0:T(8,128)S(1)}) custom-call(f32[8,8,256]{2,1,0:T(8,128)S(1)} %get-tuple-element.11.chip_half, f32[8,8,256]{2,1,0:T(8,128)S(1)} %get-tuple-element.12.far_half, ...), custom_call_target="tpu_custom_call" | custom-call | flops 8000000 | bytes 2000000 | tf_op jit(solution)/shard_map/pallas_call | solution.py:523
  7.3 0.0 collective-permute-done.1.far_got
  7.3 1.3 %shard_map.43 = (f32[16,8,128]{2,1,0:T(8,128)S(1)}, f32[2,128]{1,0:T(2,128)S(1)}, f32[15,16,24,128]{3,2,1,0:T(8,128)S(1)}) custom-call(f32[8,8,256]{2,1,0:T(8,128)S(1)} %collective-permute-done.1.far_got, f32[15,16,24,128]{3,2,1,0:T(8,128)S(1)} %get-tuple-element.14.edges, ...), custom_call_target="tpu_custom_call", output_to_operand_aliasing={{2}: (1, {})} | custom-call | tf_op jit(solution)/shard_map/pallas_call | solution.py:538
  8.7 0.3 %collective-permute-start.2 = (f32[2,128]{1,0:T(2,128)S(1)}, f32[2,128]{1,0:T(2,128)S(1)}, u32[]{:S(2)}, u32[]{:S(2)}) collective-permute-start(f32[2,128]{1,0:T(2,128)S(1)} %get-tuple-element.19), channel_id=1, source_target_pairs={{0,1},{1,0},{2,3},{3,2},{4,5},{5,4},{6,7},{7,6},{8,9},{9,8},{10,11... | collective-permute-start | bytes 3080 | tf_op jit(solution)/shard_map/ppermute | solution.py:510
  8.9 0.9 %collective-permute-done.2 = f32[2,128]{1,0:T(2,128)S(1)} collective-permute-done((f32[2,128]{1,0:T(2,128)S(1)}, f32[2,128]{1,0:T(2,128)S(1)}, u32[]{:S(2)}, u32[]{:S(2)}) %collective-permute-start.2) | collective-permute-done | bytes 1056 | tf_op jit(solution)/shard_map/ppermute | solution.py:510
  9.9 1.4 %collective-permute-start.3 = (f32[2,128]{1,0:T(2,128)S(1)}, f32[2,128]{1,0:T(2,128)S(1)}, u32[]{:S(2)}, u32[]{:S(2)}) collective-permute-start(f32[2,128]{1,0:T(2,128)S(1)} %add.6), channel_id=1, source_target_pairs={{0,5},{1,4},{2,7},{3,6},{4,1},{5,0},{6,3},{7,2},{8,13},{9,12},{10,... | collective-permute-start | bytes 3080 | tf_op jit(solution)/shard_map/ppermute | solution.py:510
  11.3 1.6 %collective-permute-done.3 = f32[2,128]{1,0:T(2,128)S(1)} collective-permute-done((f32[2,128]{1,0:T(2,128)S(1)}, f32[2,128]{1,0:T(2,128)S(1)}, u32[]{:S(2)}, u32[]{:S(2)}) %collective-permute-start.3) | collective-permute-done | bytes 1056 | tf_op jit(solution)/shard_map/ppermute | solution.py:510
  12.9 2.4 %collective-permute-start.4 = (f32[2,128]{1,0:T(2,128)S(1)}, f32[2,128]{1,0:T(2,128)S(1)}, u32[]{:S(2)}, u32[]{:S(2)}) collective-permute-start(f32[2,128]{1,0:T(2,128)S(1)} %add.7.sums), channel_id=1, source_target_pairs={{0,9},{1,8},{2,11},{3,10},{4,13},{5,12},{6,15},{7,14},{8,1},{9,0},... | collective-permute-start | bytes 3080 | tf_op jit(solution)/shard_map/ppermute | solution.py:510
  15.3 1.0 %shard_map.44 = f32[1,8,16,256]{3,2,1,0:T(8,128)} custom-call(f32[16,8,128]{2,1,0:T(8,128)S(1)} %get-tuple-element.13.near, f32[16,8,128]{2,1,0:T(8,128)S(1)} %get-tuple-element.18.far), custom_call_target="tpu_custom_call" | custom-call | tf_op jit(solution)/shard_map/pallas_call | solution.py:546
  16.2 0.5 %collective-permute-done.4.got = f32[2,128]{1,0:T(2,128)S(1)} collective-permute-done((f32[2,128]{1,0:T(2,128)S(1)}, f32[2,128]{1,0:T(2,128)S(1)}, u32[]{:S(2)}, u32[]{:S(2)}) %collective-permute-start.4) | collective-permute-done | bytes 1056 | tf_op jit(solution)/shard_map/ppermute | solution.py:510
  16.8 0.6 %shard_map.45 = f32[1,2]{1,0:T(1,128)} custom-call(f32[2,128]{1,0:T(2,128)S(1)} %add.7.sums, f32[2,128]{1,0:T(2,128)S(1)} %collective-permute-done.4.got), custom_call_target="tpu_custom_call" | custom-call | tf_op jit(solution)/shard_map/pallas_call | solution.py:561
  (3 shorter events, 0.0 us)
Async XLA Ops:
  0.6 0.9 %copy-start = (f32[8,16,256]{2,1,0:T(8,128)S(1)}, f32[8,16,256]{2,1,0:T(8,128)}, u32[]{:S(2)}) copy-start(f32[8,16,256]{2,1,0:T(8,128)} %field.1) | copy-start | bytes 393220
  1.6 3.1 %collective-permute-start = (f32[8,8,256]{2,1,0:T(8,128)S(1)}, f32[8,8,256]{2,1,0:T(8,128)S(1)}, u32[]{:S(2)}, u32[]{:S(2)}) collective-permute-start(f32[8,8,256]{2,1,0:T(8,128)S(1)} %get-tuple-element.11.chip_half), channel_id=1, source_target_pairs={{0,1},{1,0},{2,3},{3,2},{4,5},{5,4},{6,7},{7,6},{8,9},{9,8},{10,11... | collective-permute-start | bytes 196616 | tf_op jit(solution)/shard_map/ppermute | solution.py:510
  2.1 5.2 %collective-permute-start.1 = (f32[8,8,256]{2,1,0:T(8,128)S(1)}, f32[8,8,256]{2,1,0:T(8,128)S(1)}, u32[]{:S(2)}, u32[]{:S(2)}) collective-permute-start(f32[8,8,256]{2,1,0:T(8,128)S(1)} %get-tuple-element.12.far_half), channel_id=1, source_target_pairs={{0,2},{1,4},{2,0},{3,6},{4,1},{5,8},{6,3},{7,10},{8,5},{9,12},{10,... | collective-permute-start | bytes 196616 | tf_op jit(solution)/shard_map/ppermute | solution.py:510
  4.7 0.7 %copy-start.1 = (s32[8,6]{1,0:T(8,128)S(1)}, s32[8,6]{1,0:T(8,128)}, u32[]{:S(2)}) copy-start(s32[8,6]{1,0:T(8,128)} %table.1) | copy-start | bytes 580
  8.7 1.2 %collective-permute-start.2 = (f32[2,128]{1,0:T(2,128)S(1)}, f32[2,128]{1,0:T(2,128)S(1)}, u32[]{:S(2)}, u32[]{:S(2)}) collective-permute-start(f32[2,128]{1,0:T(2,128)S(1)} %get-tuple-element.19), channel_id=1, source_target_pairs={{0,1},{1,0},{2,3},{3,2},{4,5},{5,4},{6,7},{7,6},{8,9},{9,8},{10,11... | collective-permute-start | bytes 3080 | tf_op jit(solution)/shard_map/ppermute | solution.py:510
  9.9 3.0 %collective-permute-start.3 = (f32[2,128]{1,0:T(2,128)S(1)}, f32[2,128]{1,0:T(2,128)S(1)}, u32[]{:S(2)}, u32[]{:S(2)}) collective-permute-start(f32[2,128]{1,0:T(2,128)S(1)} %add.6), channel_id=1, source_target_pairs={{0,5},{1,4},{2,7},{3,6},{4,1},{5,0},{6,3},{7,2},{8,13},{9,12},{10,... | collective-permute-start | bytes 3080 | tf_op jit(solution)/shard_map/ppermute | solution.py:510
  12.9 3.9 %collective-permute-start.4 = (f32[2,128]{1,0:T(2,128)S(1)}, f32[2,128]{1,0:T(2,128)S(1)}, u32[]{:S(2)}, u32[]{:S(2)}) collective-permute-start(f32[2,128]{1,0:T(2,128)S(1)} %add.7.sums), channel_id=1, source_target_pairs={{0,9},{1,8},{2,11},{3,10},{4,13},{5,12},{6,15},{7,14},{8,1},{9,0},... | collective-permute-start | bytes 3080 | tf_op jit(solution)/shard_map/ppermute | solution.py:510

commit v5 on v4

--- a/solution.py
+++ b/solution.py
@@ -219,7 +219,8 @@
         return jnp.where(inner, picked(other, lanes), own)
 
     cells = [center(cell) for cell in range(CELLS)]
-    for cell in range(CELLS):
+    rim = [cell for cell in range(CELLS) if cell // 4 in (0, 3) or cell % 4 in (0, 3)]
+    for cell in rim + [5, 6, 9, 10]:
         value = cells[cell]
         inner_j, inner_k = cell // 4, cell % 4
         total = side_a(cell) + side_b(cell)
@@ -458,8 +459,13 @@
         second_squares.append(change * change)
         change = earlier - state[0, cell, shifted(level)]
         first_squares.append(change * change)
-    sums[0:1, :] = jnp.sum(added(first_squares), axis=0, keepdims=True)
-    sums[1:2, :] = jnp.sum(added(second_squares), axis=0, keepdims=True)
+    first, second = added(first_squares), added(second_squares)
+    row = lax.broadcasted_iota(jnp.int32, (8, LANES), 0)
+    both = jnp.where(row < 4, first + pltpu.roll(first, 4, 0), second + pltpu.roll(second, 4, 0))
+    both = both + pltpu.roll(both, 6, 0)
+    both = both + pltpu.roll(both, 7, 0)
+    sums[0:1, :] = both[0:1]
+    sums[1:2, :] = both[4:5]
 
 
 def norm_kernel(cells, sums, got, norms):

time: 17.5 us -> 17.5 us (level)
  no operation moved by 1% of the time
where the time goes in v5:
time: 17.5 us; the launch traced here: 17.3 us
  starting transfers between devices  7.12 us (41%)
  Pallas kernels  4.85 us (28%)
  waiting for transfers between devices  3.09 us (18%)
  local copies, waits for them, and re-layouts  1.58 us (9%)
  between operations  0.67 us (4%)
    ppermute x5, starting transfers between devices, moved(): return lax.ppermute(value, axes, pairs_over(sizes, partner))  7.12 us
    ppermute x5, waiting for transfers between devices, moved(): return lax.ppermute(value, axes, pairs_over(sizes, partner))  3.09 us
    pallas_call x1, Pallas kernels, shards(): pl.pallas_call(functools.partial(near_kernel, scheme), out_shape=[shared,...  1.96 us
    unnamed x4, local copies, waits for them, and re-layouts  1.58 us
    pallas_call x1, Pallas kernels, shards(): pl.pallas_call(functools.partial(far_kernel, scheme), out_shape=[planes,...  1.29 us
    pallas_call x1, Pallas kernels, shards(): pl.pallas_call(merge_kernel, out_shape=jax.ShapeDtypeStruct((1, 8, EDGE,...  0.96 us
    pallas_call x1, Pallas kernels, shards(): pl.pallas_call(functools.partial(norm_kernel, np.float32(cells)), out_sha...  0.6 us
  transfers between devices with their start and end apart: 5, of which 3 were waited for; matrix products, arithmetic and copies ran while one was open for 0% of the time, Pallas kernels for 17%

profile of v5, /device:TPU:0, one launch (start us, length us, event | category | flops | bytes accessed | tf_op | source)
XLA Modules:
  0.0 17.3 jit_solution(1775091921312975658)
XLA Ops:
  0.6 0.0 copy-start
  0.6 0.9 %copy-done = f32[8,16,256]{2,1,0:T(8,128)S(1)} copy-done((f32[8,16,256]{2,1,0:T(8,128)S(1)}, f32[8,16,256]{2,1,0:T(8,128)}, u32[]{:S(2)}) %copy-start) | copy-done | bytes 131096
  1.6 0.5 %collective-permute-start = (f32[8,8,256]{2,1,0:T(8,128)S(1)}, f32[8,8,256]{2,1,0:T(8,128)S(1)}, u32[]{:S(2)}, u32[]{:S(2)}) collective-permute-start(f32[8,8,256]{2,1,0:T(8,128)S(1)} %get-tuple-element.11.chip_half), channel_id=1, source_target_pairs={{0,1},{1,0},{2,3},{3,2},{4,5},{5,4},{6,7},{7,6},{8,9},{9,8},{10,11... | collective-permute-start | bytes 196616 | tf_op jit(solution)/shard_map/ppermute | solution.py:516
  2.1 2.6 %collective-permute-start.1 = (f32[8,8,256]{2,1,0:T(8,128)S(1)}, f32[8,8,256]{2,1,0:T(8,128)S(1)}, u32[]{:S(2)}, u32[]{:S(2)}) collective-permute-start(f32[8,8,256]{2,1,0:T(8,128)S(1)} %get-tuple-element.12.far_half), channel_id=1, source_target_pairs={{0,2},{1,4},{2,0},{3,6},{4,1},{5,8},{6,3},{7,10},{8,5},{9,12},{10,... | collective-permute-start | bytes 196616 | tf_op jit(solution)/shard_map/ppermute | solution.py:516
  4.7 0.0 collective-permute-done.chip_got
  4.7 0.0 copy-start.1
  4.7 0.7 %copy-done.1 = s32[8,6]{1,0:T(8,128)S(1)} copy-done((s32[8,6]{1,0:T(8,128)S(1)}, s32[8,6]{1,0:T(8,128)}, u32[]{:S(2)}) %copy-start.1) | copy-done | bytes 216
  5.4 2.0 %shard_map.42 = (f32[15,16,24,128]{3,2,1,0:T(8,128)S(1)}, f32[16,8,128]{2,1,0:T(8,128)S(1)}, f32[16,8,128]{2,1,0:T(8,128)S(1)}, f32[2,8,128]{2,1,0:T(8,128)S(1)}, s32[6,8,128]{2,1,0:T(8,128)S(1)}) custom-call(f32[8,8,256]{2,1,0:T(8,128)S(1)} %get-tuple-element.11.chip_half, f32[8,8,256]{2,1,0:T(8,128)S(1)} %get-tuple-element.12.far_half, ...), custom_call_target="tpu_custom_call" | custom-call | flops 8000000 | bytes 2000000 | tf_op jit(solution)/shard_map/pallas_call | solution.py:529
  7.3 0.0 collective-permute-done.1.far_got
  7.3 1.3 %shard_map.43 = (f32[16,8,128]{2,1,0:T(8,128)S(1)}, f32[2,128]{1,0:T(2,128)S(1)}, f32[15,16,24,128]{3,2,1,0:T(8,128)S(1)}) custom-call(f32[8,8,256]{2,1,0:T(8,128)S(1)} %collective-permute-done.1.far_got, f32[15,16,24,128]{3,2,1,0:T(8,128)S(1)} %get-tuple-element.14.edges, ...), custom_call_target="tpu_custom_call", output_to_operand_aliasing={{2}: (1, {})} | custom-call | tf_op jit(solution)/shard_map/pallas_call | solution.py:544
  8.6 0.3 %collective-permute-start.2 = (f32[2,128]{1,0:T(2,128)S(1)}, f32[2,128]{1,0:T(2,128)S(1)}, u32[]{:S(2)}, u32[]{:S(2)}) collective-permute-start(f32[2,128]{1,0:T(2,128)S(1)} %get-tuple-element.19), channel_id=1, source_target_pairs={{0,1},{1,0},{2,3},{3,2},{4,5},{5,4},{6,7},{7,6},{8,9},{9,8},{10,11... | collective-permute-start | bytes 3080 | tf_op jit(solution)/shard_map/ppermute | solution.py:516
  8.9 0.9 %collective-permute-done.2 = f32[2,128]{1,0:T(2,128)S(1)} collective-permute-done((f32[2,128]{1,0:T(2,128)S(1)}, f32[2,128]{1,0:T(2,128)S(1)}, u32[]{:S(2)}, u32[]{:S(2)}) %collective-permute-start.2) | collective-permute-done | bytes 1056 | tf_op jit(solution)/shard_map/ppermute | solution.py:516
  9.8 1.4 %collective-permute-start.3 = (f32[2,128]{1,0:T(2,128)S(1)}, f32[2,128]{1,0:T(2,128)S(1)}, u32[]{:S(2)}, u32[]{:S(2)}) collective-permute-start(f32[2,128]{1,0:T(2,128)S(1)} %add.6), channel_id=1, source_target_pairs={{0,5},{1,4},{2,7},{3,6},{4,1},{5,0},{6,3},{7,2},{8,13},{9,12},{10,... | collective-permute-start | bytes 3080 | tf_op jit(solution)/shard_map/ppermute | solution.py:516
  11.2 1.6 %collective-permute-done.3 = f32[2,128]{1,0:T(2,128)S(1)} collective-permute-done((f32[2,128]{1,0:T(2,128)S(1)}, f32[2,128]{1,0:T(2,128)S(1)}, u32[]{:S(2)}, u32[]{:S(2)}) %collective-permute-start.3) | collective-permute-done | bytes 1056 | tf_op jit(solution)/shard_map/ppermute | solution.py:516
  12.8 2.4 %collective-permute-start.4 = (f32[2,128]{1,0:T(2,128)S(1)}, f32[2,128]{1,0:T(2,128)S(1)}, u32[]{:S(2)}, u32[]{:S(2)}) collective-permute-start(f32[2,128]{1,0:T(2,128)S(1)} %add.7.sums), channel_id=1, source_target_pairs={{0,9},{1,8},{2,11},{3,10},{4,13},{5,12},{6,15},{7,14},{8,1},{9,0},... | collective-permute-start | bytes 3080 | tf_op jit(solution)/shard_map/ppermute | solution.py:516
  15.2 1.0 %shard_map.44 = f32[1,8,16,256]{3,2,1,0:T(8,128)} custom-call(f32[16,8,128]{2,1,0:T(8,128)S(1)} %get-tuple-element.13.near, f32[16,8,128]{2,1,0:T(8,128)S(1)} %get-tuple-element.18.far), custom_call_target="tpu_custom_call" | custom-call | tf_op jit(solution)/shard_map/pallas_call | solution.py:552
  16.2 0.5 %collective-permute-done.4.got = f32[2,128]{1,0:T(2,128)S(1)} collective-permute-done((f32[2,128]{1,0:T(2,128)S(1)}, f32[2,128]{1,0:T(2,128)S(1)}, u32[]{:S(2)}, u32[]{:S(2)}) %collective-permute-start.4) | collective-permute-done | bytes 1056 | tf_op jit(solution)/shard_map/ppermute | solution.py:516
  16.7 0.6 %shard_map.45 = f32[1,2]{1,0:T(1,128)} custom-call(f32[2,128]{1,0:T(2,128)S(1)} %add.7.sums, f32[2,128]{1,0:T(2,128)S(1)} %collective-permute-done.4.got), custom_call_target="tpu_custom_call" | custom-call | tf_op jit(solution)/shard_map/pallas_call | solution.py:567
  (3 shorter events, 0.0 us)
Async XLA Ops:
  0.6 0.9 %copy-start = (f32[8,16,256]{2,1,0:T(8,128)S(1)}, f32[8,16,256]{2,1,0:T(8,128)}, u32[]{:S(2)}) copy-start(f32[8,16,256]{2,1,0:T(8,128)} %field.1) | copy-start | bytes 393220
  1.6 3.1 %collective-permute-start = (f32[8,8,256]{2,1,0:T(8,128)S(1)}, f32[8,8,256]{2,1,0:T(8,128)S(1)}, u32[]{:S(2)}, u32[]{:S(2)}) collective-permute-start(f32[8,8,256]{2,1,0:T(8,128)S(1)} %get-tuple-element.11.chip_half), channel_id=1, source_target_pairs={{0,1},{1,0},{2,3},{3,2},{4,5},{5,4},{6,7},{7,6},{8,9},{9,8},{10,11... | collective-permute-start | bytes 196616 | tf_op jit(solution)/shard_map/ppermute | solution.py:516
  2.1 5.2 %collective-permute-start.1 = (f32[8,8,256]{2,1,0:T(8,128)S(1)}, f32[8,8,256]{2,1,0:T(8,128)S(1)}, u32[]{:S(2)}, u32[]{:S(2)}) collective-permute-start(f32[8,8,256]{2,1,0:T(8,128)S(1)} %get-tuple-element.12.far_half), channel_id=1, source_target_pairs={{0,2},{1,4},{2,0},{3,6},{4,1},{5,8},{6,3},{7,10},{8,5},{9,12},{10,... | collective-permute-start | bytes 196616 | tf_op jit(solution)/shard_map/ppermute | solution.py:516
  4.7 0.7 %copy-start.1 = (s32[8,6]{1,0:T(8,128)S(1)}, s32[8,6]{1,0:T(8,128)}, u32[]{:S(2)}) copy-start(s32[8,6]{1,0:T(8,128)} %table.1) | copy-start | bytes 580
  8.6 1.2 %collective-permute-start.2 = (f32[2,128]{1,0:T(2,128)S(1)}, f32[2,128]{1,0:T(2,128)S(1)}, u32[]{:S(2)}, u32[]{:S(2)}) collective-permute-start(f32[2,128]{1,0:T(2,128)S(1)} %get-tuple-element.19), channel_id=1, source_target_pairs={{0,1},{1,0},{2,3},{3,2},{4,5},{5,4},{6,7},{7,6},{8,9},{9,8},{10,11... | collective-permute-start | bytes 3080 | tf_op jit(solution)/shard_map/ppermute | solution.py:516
  9.8 3.0 %collective-permute-start.3 = (f32[2,128]{1,0:T(2,128)S(1)}, f32[2,128]{1,0:T(2,128)S(1)}, u32[]{:S(2)}, u32[]{:S(2)}) collective-permute-start(f32[2,128]{1,0:T(2,128)S(1)} %add.6), channel_id=1, source_target_pairs={{0,5},{1,4},{2,7},{3,6},{4,1},{5,0},{6,3},{7,2},{8,13},{9,12},{10,... | collective-permute-start | bytes 3080 | tf_op jit(solution)/shard_map/ppermute | solution.py:516
  12.8 3.9 %collective-permute-start.4 = (f32[2,128]{1,0:T(2,128)S(1)}, f32[2,128]{1,0:T(2,128)S(1)}, u32[]{:S(2)}, u32[]{:S(2)}) collective-permute-start(f32[2,128]{1,0:T(2,128)S(1)} %add.7.sums), channel_id=1, source_target_pairs={{0,9},{1,8},{2,11},{3,10},{4,13},{5,12},{6,15},{7,14},{8,1},{9,0},... | collective-permute-start | bytes 3080 | tf_op jit(solution)/shard_map/ppermute | solution.py:516

commit v6 on v4

--- a/solution.py
+++ b/solution.py
@@ -485,24 +485,24 @@
 
 def shards(start_field, neighbours):
     nodes = lax.axis_size("node")
-    axes = ("curve", "node", "sub")
+    axes = ("slab", "curve", "node", "sub")
     sizes = tuple(lax.axis_size(axis) for axis in axes)
-    chips = sizes[0]
+    chips = sizes[1]
     scheme = Scheme(nodes, *radau_tables(nodes))
     half = jax.ShapeDtypeStruct((8, 8, EDGE * EDGE), jnp.float32)
     planes = jax.ShapeDtypeStruct((CELLS, 8, LANES), jnp.float32)
     limit = pltpu.CompilerParams(vmem_limit_bytes=24 * 1024 * 1024)
 
-    def across(curve, node, sub):
+    def across(slab, curve, node, sub):
         if sub == 1 and curve + 1 < chips:
-            return (curve + 1, node, 0)
+            return (slab, curve + 1, node, 0)
         if sub == 0 and curve > 0:
-            return (curve - 1, node, 1)
-        return (curve, node ^ 1, sub) if node ^ 1 < nodes else None
+            return (slab, curve - 1, node, 1)
+        return (slab ^ 1, curve, node, sub) if slab ^ 1 < sizes[0] else None
 
     def beside(bit, swap):
-        def partner(curve, node, sub):
-            return (curve ^ bit, node, sub ^ swap)
+        def partner(slab, curve, node, sub):
+            return (slab, curve ^ bit, node, sub ^ swap)
 
         return partner
 
@@ -557,7 +557,7 @@
         bit *= 2
     for partner in rounds[:-1]:
         sums = sums + moved(sums, partner)
-    cells = start_field.size * chips * sizes[2]
+    cells = start_field.size * chips * sizes[3]
     increments = pl.pallas_call(
         functools.partial(norm_kernel, np.float32(cells)),
         out_shape=jax.ShapeDtypeStruct((1, SWEEPS), jnp.float32),

time: 17.5 us -> 17.6 us (level)
  no operation moved by 1% of the time
where the time goes in v6:
time: 17.6 us; the launch traced here: 17.4 us
  starting transfers between devices  7.08 us (40%)
  Pallas kernels  4.88 us (28%)
  waiting for transfers between devices  3.16 us (18%)
  local copies, waits for them, and re-layouts  1.58 us (9%)
  between operations  0.67 us (4%)
    ppermute x5, starting transfers between devices, moved(): return lax.ppermute(value, axes, pairs_over(sizes, partner))  7.08 us
    ppermute x5, waiting for transfers between devices, moved(): return lax.ppermute(value, axes, pairs_over(sizes, partner))  3.16 us
    pallas_call x1, Pallas kernels, shards(): pl.pallas_call(functools.partial(near_kernel, scheme), out_shape=[shared,...  1.95 us
    unnamed x4, local copies, waits for them, and re-layouts  1.58 us
    pallas_call x1, Pallas kernels, shards(): pl.pallas_call(functools.partial(far_kernel, scheme), out_shape=[planes,...  1.32 us
    pallas_call x1, Pallas kernels, shards(): pl.pallas_call(merge_kernel, out_shape=jax.ShapeDtypeStruct((1, 8, EDGE,...  0.96 us
    pallas_call x1, Pallas kernels, shards(): pl.pallas_call(functools.partial(norm_kernel, np.float32(cells)), out_sha...  0.6 us
  transfers between devices with their start and end apart: 5, of which 3 were waited for; matrix products, arithmetic and copies ran while one was open for 0% of the time, Pallas kernels for 17%

profile of v6, /device:TPU:0, one launch (start us, length us, event | category | flops | bytes accessed | tf_op | source)
XLA Modules:
  0.0 17.4 jit_solution(6472003365131577173)
XLA Ops:
  0.6 0.0 copy-start
  0.6 0.9 %copy-done = f32[8,16,256]{2,1,0:T(8,128)S(1)} copy-done((f32[8,16,256]{2,1,0:T(8,128)S(1)}, f32[8,16,256]{2,1,0:T(8,128)}, u32[]{:S(2)}) %copy-start) | copy-done | bytes 131096
  1.6 0.5 %collective-permute-start = (f32[8,8,256]{2,1,0:T(8,128)S(1)}, f32[8,8,256]{2,1,0:T(8,128)S(1)}, u32[]{:S(2)}, u32[]{:S(2)}) collective-permute-start(f32[8,8,256]{2,1,0:T(8,128)S(1)} %get-tuple-element.11.chip_half), channel_id=1, source_target_pairs={{0,1},{1,0},{2,3},{3,2},{4,5},{5,4},{6,7},{7,6},{8,9},{9,8},{10,11... | collective-permute-start | bytes 196616 | tf_op jit(solution)/shard_map/ppermute | solution.py:510
  2.1 2.6 %collective-permute-start.1 = (f32[8,8,256]{2,1,0:T(8,128)S(1)}, f32[8,8,256]{2,1,0:T(8,128)S(1)}, u32[]{:S(2)}, u32[]{:S(2)}) collective-permute-start(f32[8,8,256]{2,1,0:T(8,128)S(1)} %get-tuple-element.12.far_half), channel_id=1, source_target_pairs={{0,16},{1,4},{2,18},{3,6},{4,1},{5,8},{6,3},{7,10},{8,5},{9,12},{1... | collective-permute-start | bytes 196616 | tf_op jit(solution)/shard_map/ppermute | solution.py:510
  4.7 0.0 collective-permute-done.chip_got
  4.7 0.0 copy-start.1
  4.7 0.7 %copy-done.1 = s32[8,6]{1,0:T(8,128)S(1)} copy-done((s32[8,6]{1,0:T(8,128)S(1)}, s32[8,6]{1,0:T(8,128)}, u32[]{:S(2)}) %copy-start.1) | copy-done | bytes 216
  5.4 2.0 %shard_map.42 = (f32[15,16,24,128]{3,2,1,0:T(8,128)S(1)}, f32[16,8,128]{2,1,0:T(8,128)S(1)}, f32[16,8,128]{2,1,0:T(8,128)S(1)}, f32[2,8,128]{2,1,0:T(8,128)S(1)}, s32[6,8,128]{2,1,0:T(8,128)S(1)}) custom-call(f32[8,8,256]{2,1,0:T(8,128)S(1)} %get-tuple-element.11.chip_half, f32[8,8,256]{2,1,0:T(8,128)S(1)} %get-tuple-element.12.far_half, ...), custom_call_target="tpu_custom_call" | custom-call | flops 8000000 | bytes 2000000 | tf_op jit(solution)/shard_map/pallas_call | solution.py:523
  7.3 0.0 collective-permute-done.1.far_got
  7.4 1.3 %shard_map.43 = (f32[16,8,128]{2,1,0:T(8,128)S(1)}, f32[2,128]{1,0:T(2,128)S(1)}, f32[15,16,24,128]{3,2,1,0:T(8,128)S(1)}) custom-call(f32[8,8,256]{2,1,0:T(8,128)S(1)} %collective-permute-done.1.far_got, f32[15,16,24,128]{3,2,1,0:T(8,128)S(1)} %get-tuple-element.14.edges, ...), custom_call_target="tpu_custom_call", output_to_operand_aliasing={{2}: (1, {})} | custom-call | tf_op jit(solution)/shard_map/pallas_call | solution.py:538
  8.7 0.2 %collective-permute-start.2 = (f32[2,128]{1,0:T(2,128)S(1)}, f32[2,128]{1,0:T(2,128)S(1)}, u32[]{:S(2)}, u32[]{:S(2)}) collective-permute-start(f32[2,128]{1,0:T(2,128)S(1)} %get-tuple-element.19), channel_id=1, source_target_pairs={{0,1},{1,0},{2,3},{3,2},{4,5},{5,4},{6,7},{7,6},{8,9},{9,8},{10,11... | collective-permute-start | bytes 3080 | tf_op jit(solution)/shard_map/ppermute | solution.py:510
  8.9 1.0 %collective-permute-done.2 = f32[2,128]{1,0:T(2,128)S(1)} collective-permute-done((f32[2,128]{1,0:T(2,128)S(1)}, f32[2,128]{1,0:T(2,128)S(1)}, u32[]{:S(2)}, u32[]{:S(2)}) %collective-permute-start.2) | collective-permute-done | bytes 1056 | tf_op jit(solution)/shard_map/ppermute | solution.py:510
  9.9 1.4 %collective-permute-start.3 = (f32[2,128]{1,0:T(2,128)S(1)}, f32[2,128]{1,0:T(2,128)S(1)}, u32[]{:S(2)}, u32[]{:S(2)}) collective-permute-start(f32[2,128]{1,0:T(2,128)S(1)} %add.6), channel_id=1, source_target_pairs={{0,5},{1,4},{2,7},{3,6},{4,1},{5,0},{6,3},{7,2},{8,13},{9,12},{10,... | collective-permute-start | bytes 3080 | tf_op jit(solution)/shard_map/ppermute | solution.py:510
  11.3 1.6 %collective-permute-done.3 = f32[2,128]{1,0:T(2,128)S(1)} collective-permute-done((f32[2,128]{1,0:T(2,128)S(1)}, f32[2,128]{1,0:T(2,128)S(1)}, u32[]{:S(2)}, u32[]{:S(2)}) %collective-permute-start.3) | collective-permute-done | bytes 1056 | tf_op jit(solution)/shard_map/ppermute | solution.py:510
  12.9 2.4 %collective-permute-start.4 = (f32[2,128]{1,0:T(2,128)S(1)}, f32[2,128]{1,0:T(2,128)S(1)}, u32[]{:S(2)}, u32[]{:S(2)}) collective-permute-start(f32[2,128]{1,0:T(2,128)S(1)} %add.7.sums), channel_id=1, source_target_pairs={{0,9},{1,8},{2,11},{3,10},{4,13},{5,12},{6,15},{7,14},{8,1},{9,0},... | collective-permute-start | bytes 3080 | tf_op jit(solution)/shard_map/ppermute | solution.py:510
  15.3 1.0 %shard_map.44 = f32[1,8,16,256]{3,2,1,0:T(8,128)} custom-call(f32[16,8,128]{2,1,0:T(8,128)S(1)} %get-tuple-element.13.near, f32[16,8,128]{2,1,0:T(8,128)S(1)} %get-tuple-element.18.far), custom_call_target="tpu_custom_call" | custom-call | tf_op jit(solution)/shard_map/pallas_call | solution.py:546
  16.2 0.6 %collective-permute-done.4.got = f32[2,128]{1,0:T(2,128)S(1)} collective-permute-done((f32[2,128]{1,0:T(2,128)S(1)}, f32[2,128]{1,0:T(2,128)S(1)}, u32[]{:S(2)}, u32[]{:S(2)}) %collective-permute-start.4) | collective-permute-done | bytes 1056 | tf_op jit(solution)/shard_map/ppermute | solution.py:510
  16.8 0.6 %shard_map.45 = f32[1,2]{1,0:T(1,128)} custom-call(f32[2,128]{1,0:T(2,128)S(1)} %add.7.sums, f32[2,128]{1,0:T(2,128)S(1)} %collective-permute-done.4.got), custom_call_target="tpu_custom_call" | custom-call | tf_op jit(solution)/shard_map/pallas_call | solution.py:561
  (3 shorter events, 0.0 us)
Async XLA Ops:
  0.6 0.9 %copy-start = (f32[8,16,256]{2,1,0:T(8,128)S(1)}, f32[8,16,256]{2,1,0:T(8,128)}, u32[]{:S(2)}) copy-start(f32[8,16,256]{2,1,0:T(8,128)} %field.1) | copy-start | bytes 393220
  1.6 3.1 %collective-permute-start = (f32[8,8,256]{2,1,0:T(8,128)S(1)}, f32[8,8,256]{2,1,0:T(8,128)S(1)}, u32[]{:S(2)}, u32[]{:S(2)}) collective-permute-start(f32[8,8,256]{2,1,0:T(8,128)S(1)} %get-tuple-element.11.chip_half), channel_id=1, source_target_pairs={{0,1},{1,0},{2,3},{3,2},{4,5},{5,4},{6,7},{7,6},{8,9},{9,8},{10,11... | collective-permute-start | bytes 196616 | tf_op jit(solution)/shard_map/ppermute | solution.py:510
  2.1 5.2 %collective-permute-start.1 = (f32[8,8,256]{2,1,0:T(8,128)S(1)}, f32[8,8,256]{2,1,0:T(8,128)S(1)}, u32[]{:S(2)}, u32[]{:S(2)}) collective-permute-start(f32[8,8,256]{2,1,0:T(8,128)S(1)} %get-tuple-element.12.far_half), channel_id=1, source_target_pairs={{0,16},{1,4},{2,18},{3,6},{4,1},{5,8},{6,3},{7,10},{8,5},{9,12},{1... | collective-permute-start | bytes 196616 | tf_op jit(solution)/shard_map/ppermute | solution.py:510
  4.7 0.7 %copy-start.1 = (s32[8,6]{1,0:T(8,128)S(1)}, s32[8,6]{1,0:T(8,128)}, u32[]{:S(2)}) copy-start(s32[8,6]{1,0:T(8,128)} %table.1) | copy-start | bytes 580
  8.7 1.2 %collective-permute-start.2 = (f32[2,128]{1,0:T(2,128)S(1)}, f32[2,128]{1,0:T(2,128)S(1)}, u32[]{:S(2)}, u32[]{:S(2)}) collective-permute-start(f32[2,128]{1,0:T(2,128)S(1)} %get-tuple-element.19), channel_id=1, source_target_pairs={{0,1},{1,0},{2,3},{3,2},{4,5},{5,4},{6,7},{7,6},{8,9},{9,8},{10,11... | collective-permute-start | bytes 3080 | tf_op jit(solution)/shard_map/ppermute | solution.py:510
  9.9 3.0 %collective-permute-start.3 = (f32[2,128]{1,0:T(2,128)S(1)}, f32[2,128]{1,0:T(2,128)S(1)}, u32[]{:S(2)}, u32[]{:S(2)}) collective-permute-start(f32[2,128]{1,0:T(2,128)S(1)} %add.6), channel_id=1, source_target_pairs={{0,5},{1,4},{2,7},{3,6},{4,1},{5,0},{6,3},{7,2},{8,13},{9,12},{10,... | collective-permute-start | bytes 3080 | tf_op jit(solution)/shard_map/ppermute | solution.py:510
  12.9 3.9 %collective-permute-start.4 = (f32[2,128]{1,0:T(2,128)S(1)}, f32[2,128]{1,0:T(2,128)S(1)}, u32[]{:S(2)}, u32[]{:S(2)}) collective-permute-start(f32[2,128]{1,0:T(2,128)S(1)} %add.7.sums), channel_id=1, source_target_pairs={{0,9},{1,8},{2,11},{3,10},{4,13},{5,12},{6,15},{7,14},{8,1},{9,0},... | collective-permute-start | bytes 3080 | tf_op jit(solution)/shard_map/ppermute | solution.py:510

commit v7 on v4

--- a/solution.py
+++ b/solution.py
@@ -515,7 +515,7 @@
         in_specs=[pl.BlockSpec(memory_space=pltpu.HBM)],
         out_specs=[VMEM, VMEM],
         scratch_shapes=[pltpu.SemaphoreType.DMA, pltpu.SemaphoreType.DMA],
-        compiler_params=limit,
+        compiler_params=pltpu.CompilerParams(vmem_limit_bytes=55040 * 1024),
     )(start_field)
     far_got = moved(far_half, across)
     chip_got = moved(chip_half, beside(0, 1))

time: 17.5 us -> 17.5 us (level)
  local copies, waits for them, and re-layouts: 1.58 us -> 0.69 us
  Pallas kernels: 4.88 us -> 5.73 us
    unnamed x4 -> x2, local copies, waits for them, and re-layouts: 1.58 us -> 0.69 us
    pallas_call x1, Pallas kernels: 0.04 us -> 0.9 us  [shards(): pl.pallas_call(halves_kernel, out_shape=[half, half], in_specs=[pl.BlockS...]
where the time goes in v7:
time: 17.5 us; the launch traced here: 17.3 us
  starting transfers between devices  7.14 us (41%)
  Pallas kernels  5.73 us (33%)
  waiting for transfers between devices  3.08 us (18%)
  local copies, waits for them, and re-layouts  0.69 us (4%)
  between operations  0.67 us (4%)
    ppermute x5, starting transfers between devices, moved(): return lax.ppermute(value, axes, pairs_over(sizes, partner))  7.14 us
    ppermute x5, waiting for transfers between devices, moved(): return lax.ppermute(value, axes, pairs_over(sizes, partner))  3.08 us
    pallas_call x1, Pallas kernels, shards(): pl.pallas_call(functools.partial(near_kernel, scheme), out_shape=[shared,...  1.95 us
    pallas_call x1, Pallas kernels, shards(): pl.pallas_call(functools.partial(far_kernel, scheme), out_shape=[planes,...  1.32 us
    pallas_call x1, Pallas kernels, shards(): pl.pallas_call(merge_kernel, out_shape=jax.ShapeDtypeStruct((1, 8, EDGE,...  0.96 us
    pallas_call x1, Pallas kernels, shards(): pl.pallas_call(halves_kernel, out_shape=[half, half], in_specs=[pl.BlockS...  0.9 us
    unnamed x2, local copies, waits for them, and re-layouts  0.69 us
    pallas_call x1, Pallas kernels, shards(): pl.pallas_call(functools.partial(norm_kernel, np.float32(cells)), out_sha...  0.6 us
  transfers between devices with their start and end apart: 5, of which 3 were waited for; matrix products, arithmetic and copies ran while one was open for 0% of the time, Pallas kernels for 17%

profile of v7, /device:TPU:0, one launch (start us, length us, event | category | flops | bytes accessed | tf_op | source)
XLA Modules:
  0.0 17.3 jit_solution(6937902565283511229)
XLA Ops:
  0.6 0.9 %shard_map.41 = (f32[8,8,256]{2,1,0:T(8,128)S(1)}, f32[8,8,256]{2,1,0:T(8,128)S(1)}) custom-call(f32[8,16,256]{2,1,0:T(8,128)} %field.1), custom_call_target="tpu_custom_call" | custom-call | tf_op jit(solution)/shard_map/pallas_call | solution.py:512
  1.5 0.5 %collective-permute-start = (f32[8,8,256]{2,1,0:T(8,128)S(1)}, f32[8,8,256]{2,1,0:T(8,128)S(1)}, u32[]{:S(2)}, u32[]{:S(2)}) collective-permute-start(f32[8,8,256]{2,1,0:T(8,128)S(1)} %get-tuple-element.11.chip_half), channel_id=1, source_target_pairs={{0,1},{1,0},{2,3},{3,2},{4,5},{5,4},{6,7},{7,6},{8,9},{9,8},{10,11... | collective-permute-start | bytes 196616 | tf_op jit(solution)/shard_map/ppermute | solution.py:510
  2.1 2.6 %collective-permute-start.1 = (f32[8,8,256]{2,1,0:T(8,128)S(1)}, f32[8,8,256]{2,1,0:T(8,128)S(1)}, u32[]{:S(2)}, u32[]{:S(2)}) collective-permute-start(f32[8,8,256]{2,1,0:T(8,128)S(1)} %get-tuple-element.12.far_half), channel_id=1, source_target_pairs={{0,2},{1,4},{2,0},{3,6},{4,1},{5,8},{6,3},{7,10},{8,5},{9,12},{10,... | collective-permute-start | bytes 196616 | tf_op jit(solution)/shard_map/ppermute | solution.py:510
  4.6 0.0 collective-permute-done.chip_got
  4.6 0.0 copy-start
  4.6 0.7 %copy-done = s32[8,6]{1,0:T(8,128)S(1)} copy-done((s32[8,6]{1,0:T(8,128)S(1)}, s32[8,6]{1,0:T(8,128)}, u32[]{:S(2)}) %copy-start) | copy-done | bytes 216
  5.3 2.0 %shard_map.42 = (f32[15,16,24,128]{3,2,1,0:T(8,128)S(1)}, f32[16,8,128]{2,1,0:T(8,128)S(1)}, f32[16,8,128]{2,1,0:T(8,128)S(1)}, f32[2,8,128]{2,1,0:T(8,128)S(1)}, s32[6,8,128]{2,1,0:T(8,128)S(1)}) custom-call(f32[8,8,256]{2,1,0:T(8,128)S(1)} %get-tuple-element.11.chip_half, f32[8,8,256]{2,1,0:T(8,128)S(1)} %get-tuple-element.12.far_half, ...), custom_call_target="tpu_custom_call" | custom-call | flops 8000000 | bytes 2000000 | tf_op jit(solution)/shard_map/pallas_call | solution.py:523
  7.3 0.0 collective-permute-done.1.far_got
  7.3 1.3 %shard_map.43 = (f32[16,8,128]{2,1,0:T(8,128)S(1)}, f32[2,128]{1,0:T(2,128)S(1)}, f32[15,16,24,128]{3,2,1,0:T(8,128)S(1)}) custom-call(f32[8,8,256]{2,1,0:T(8,128)S(1)} %collective-permute-done.1.far_got, f32[15,16,24,128]{3,2,1,0:T(8,128)S(1)} %get-tuple-element.14.edges, ...), custom_call_target="tpu_custom_call", output_to_operand_aliasing={{2}: (1, {})} | custom-call | tf_op jit(solution)/shard_map/pallas_call | solution.py:538
  8.6 0.3 %collective-permute-start.2 = (f32[2,128]{1,0:T(2,128)S(1)}, f32[2,128]{1,0:T(2,128)S(1)}, u32[]{:S(2)}, u32[]{:S(2)}) collective-permute-start(f32[2,128]{1,0:T(2,128)S(1)} %get-tuple-element.19), channel_id=1, source_target_pairs={{0,1},{1,0},{2,3},{3,2},{4,5},{5,4},{6,7},{7,6},{8,9},{9,8},{10,11... | collective-permute-start | bytes 3080 | tf_op jit(solution)/shard_map/ppermute | solution.py:510
  8.9 0.9 %collective-permute-done.2 = f32[2,128]{1,0:T(2,128)S(1)} collective-permute-done((f32[2,128]{1,0:T(2,128)S(1)}, f32[2,128]{1,0:T(2,128)S(1)}, u32[]{:S(2)}, u32[]{:S(2)}) %collective-permute-start.2) | collective-permute-done | bytes 1056 | tf_op jit(solution)/shard_map/ppermute | solution.py:510
  9.8 1.4 %collective-permute-start.3 = (f32[2,128]{1,0:T(2,128)S(1)}, f32[2,128]{1,0:T(2,128)S(1)}, u32[]{:S(2)}, u32[]{:S(2)}) collective-permute-start(f32[2,128]{1,0:T(2,128)S(1)} %add.6), channel_id=1, source_target_pairs={{0,5},{1,4},{2,7},{3,6},{4,1},{5,0},{6,3},{7,2},{8,13},{9,12},{10,... | collective-permute-start | bytes 3080 | tf_op jit(solution)/shard_map/ppermute | solution.py:510
  11.2 1.6 %collective-permute-done.3 = f32[2,128]{1,0:T(2,128)S(1)} collective-permute-done((f32[2,128]{1,0:T(2,128)S(1)}, f32[2,128]{1,0:T(2,128)S(1)}, u32[]{:S(2)}, u32[]{:S(2)}) %collective-permute-start.3) | collective-permute-done | bytes 1056 | tf_op jit(solution)/shard_map/ppermute | solution.py:510
  12.8 2.4 %collective-permute-start.4 = (f32[2,128]{1,0:T(2,128)S(1)}, f32[2,128]{1,0:T(2,128)S(1)}, u32[]{:S(2)}, u32[]{:S(2)}) collective-permute-start(f32[2,128]{1,0:T(2,128)S(1)} %add.7.sums), channel_id=1, source_target_pairs={{0,9},{1,8},{2,11},{3,10},{4,13},{5,12},{6,15},{7,14},{8,1},{9,0},... | collective-permute-start | bytes 3080 | tf_op jit(solution)/shard_map/ppermute | solution.py:510
  15.2 1.0 %shard_map.44 = f32[1,8,16,256]{3,2,1,0:T(8,128)} custom-call(f32[16,8,128]{2,1,0:T(8,128)S(1)} %get-tuple-element.13.near, f32[16,8,128]{2,1,0:T(8,128)S(1)} %get-tuple-element.18.far), custom_call_target="tpu_custom_call" | custom-call | tf_op jit(solution)/shard_map/pallas_call | solution.py:546
  16.2 0.5 %collective-permute-done.4.got = f32[2,128]{1,0:T(2,128)S(1)} collective-permute-done((f32[2,128]{1,0:T(2,128)S(1)}, f32[2,128]{1,0:T(2,128)S(1)}, u32[]{:S(2)}, u32[]{:S(2)}) %collective-permute-start.4) | collective-permute-done | bytes 1056 | tf_op jit(solution)/shard_map/ppermute | solution.py:510
  16.7 0.6 %shard_map.45 = f32[1,2]{1,0:T(1,128)} custom-call(f32[2,128]{1,0:T(2,128)S(1)} %add.7.sums, f32[2,128]{1,0:T(2,128)S(1)} %collective-permute-done.4.got), custom_call_target="tpu_custom_call" | custom-call | tf_op jit(solution)/shard_map/pallas_call | solution.py:561
  (2 shorter events, 0.0 us)
Async XLA Ops:
  1.5 3.1 %collective-permute-start = (f32[8,8,256]{2,1,0:T(8,128)S(1)}, f32[8,8,256]{2,1,0:T(8,128)S(1)}, u32[]{:S(2)}, u32[]{:S(2)}) collective-permute-start(f32[8,8,256]{2,1,0:T(8,128)S(1)} %get-tuple-element.11.chip_half), channel_id=1, source_target_pairs={{0,1},{1,0},{2,3},{3,2},{4,5},{5,4},{6,7},{7,6},{8,9},{9,8},{10,11... | collective-permute-start | bytes 196616 | tf_op jit(solution)/shard_map/ppermute | solution.py:510
  2.1 5.2 %collective-permute-start.1 = (f32[8,8,256]{2,1,0:T(8,128)S(1)}, f32[8,8,256]{2,1,0:T(8,128)S(1)}, u32[]{:S(2)}, u32[]{:S(2)}) collective-permute-start(f32[8,8,256]{2,1,0:T(8,128)S(1)} %get-tuple-element.12.far_half), channel_id=1, source_target_pairs={{0,2},{1,4},{2,0},{3,6},{4,1},{5,8},{6,3},{7,10},{8,5},{9,12},{10,... | collective-permute-start | bytes 196616 | tf_op jit(solution)/shard_map/ppermute | solution.py:510
  4.6 0.7 %copy-start = (s32[8,6]{1,0:T(8,128)S(1)}, s32[8,6]{1,0:T(8,128)}, u32[]{:S(2)}) copy-start(s32[8,6]{1,0:T(8,128)} %table.1) | copy-start | bytes 580
  8.6 1.2 %collective-permute-start.2 = (f32[2,128]{1,0:T(2,128)S(1)}, f32[2,128]{1,0:T(2,128)S(1)}, u32[]{:S(2)}, u32[]{:S(2)}) collective-permute-start(f32[2,128]{1,0:T(2,128)S(1)} %get-tuple-element.19), channel_id=1, source_target_pairs={{0,1},{1,0},{2,3},{3,2},{4,5},{5,4},{6,7},{7,6},{8,9},{9,8},{10,11... | collective-permute-start | bytes 3080 | tf_op jit(solution)/shard_map/ppermute | solution.py:510
  9.8 3.0 %collective-permute-start.3 = (f32[2,128]{1,0:T(2,128)S(1)}, f32[2,128]{1,0:T(2,128)S(1)}, u32[]{:S(2)}, u32[]{:S(2)}) collective-permute-start(f32[2,128]{1,0:T(2,128)S(1)} %add.6), channel_id=1, source_target_pairs={{0,5},{1,4},{2,7},{3,6},{4,1},{5,0},{6,3},{7,2},{8,13},{9,12},{10,... | collective-permute-start | bytes 3080 | tf_op jit(solution)/shard_map/ppermute | solution.py:510
  12.8 3.9 %collective-permute-start.4 = (f32[2,128]{1,0:T(2,128)S(1)}, f32[2,128]{1,0:T(2,128)S(1)}, u32[]{:S(2)}, u32[]{:S(2)}) collective-permute-start(f32[2,128]{1,0:T(2,128)S(1)} %add.7.sums), channel_id=1, source_target_pairs={{0,9},{1,8},{2,11},{3,10},{4,13},{5,12},{6,15},{7,14},{8,1},{9,0},... | collective-permute-start | bytes 3080 | tf_op jit(solution)/shard_map/ppermute | solution.py:510
